TPU v7x, 512 devices: a whole 4x4x16 slice. The times are simulated.
512 devices in a mesh: lat: 8 (over x, core), lon: 64 (over y, z).
Axes of the slice: x: 4, y: 4, z: 16, core: 2. Of those that a mesh axis runs over, the one named last changes fastest.
Arguments:
- rhs: float32 [8, 64, 6, 16, 256], P('lat', 'lon')
- precond: float32 [8, 64, 6, 256], P('lat', 'lon'), may hold values from 0.3 to 1
- factor: bfloat16 [8, 64, 6, 256, 256], P('lat', 'lon')
- kriging: bfloat16 [8, 64, 6, 4, 256, 256], P('lat', 'lon'), may hold values from -0.1875 to 0.1875
- neighbours: int32 [8, 64, 6, 4], P('lat', 'lon'), may hold values from 0 to 3071, as said below
- owner: int32 [3072], replicated, may hold values from 0 to 3071, as said below
- counts: int32 [8, 64], P('lat', 'lon'), may hold values from 1 to 6, as said below
Outputs:
- solution: float32 [8, 64, 6, 16, 256], P('lat', 'lon')
- residual: float32 [8, 64, 6, 16, 256], P('lat', 'lon')
Inputs may be any that keep to these rules, and one draw needn't show every extreme that they name: `counts`: each region holds 1 to 6 blocks in its first slots; some region holds 6. `owner`: a permutation of 0 to 3071; block id g lives in slot owner[g] % 6 of region owner[g] // 6. `neighbours`: ids of live blocks in the same region or one of its eight adjacent regions, adjacency periodic in longitude and not in latitude.
All inputs are finite; a program needn't handle non-finite values.
Results may differ from a plain program's by a relative error of at most 0.025.
Values may be sent and summed in bfloat16 or wider, within the bound.
A program may use at most 64 MiB of HBM per device.

v0:
```python
import jax
import jax.numpy as jnp
from jax import lax
from jax.sharding import PartitionSpec as P

ITERS = 2


nugget = 1.0


def from_behind(block, axis, distance):
    devices = range(lax.axis_size(axis))
    route = [((i - distance) % len(devices), i) for i in devices]
    return lax.ppermute(block, axis, route)


def from_behind_2(value, axis, steps):
    count = lax.axis_size(axis)
    leading, last = (max(0, -steps), min(count, count - steps))
    return lax.ppermute(value, axis, [(source, source + steps) for source in range(leading, last)])


def with_halo(block, sides, width):
    for axis, dim in sides:
        count = lax.axis_size(axis)
        forward = [(i, i + 1) for i in range(count - 1)]
        forward.append((count - 1, 0))
        backward = [(target, source) for source, target in forward]
        low = lax.ppermute(
            lax.slice_in_dim(block, block.shape[dim] - width, None, axis=dim), axis, forward
        )
        high = lax.ppermute(lax.slice_in_dim(block, 0, width, axis=dim), axis, backward)
        block = jnp.concatenate([low, block, high], axis=dim)
    return block


def inner(first, second):
    return jnp.sum(first * second, axis=(0, 1, 2, 4))


def lon_back(values, offset):
    return from_behind(values.astype(jnp.bfloat16), "lon", offset).astype(values.dtype)


def lat_back(values, offset):
    return from_behind_2(values.astype(jnp.bfloat16), "lat", offset).astype(values.dtype)


def body(rhs, precond, factor, kriging, neighbours, owner, counts):
    slots = factor.shape[2]
    samples = rhs.shape[3]
    width = rhs.shape[4]
    links = kriging.shape[3]
    sectors = lax.axis_size("lon")
    my_lat = lax.axis_index("lat")
    my_lon = lax.axis_index("lon")
    live = (jnp.arange(slots) < counts[0, 0]).astype(jnp.float32)
    source = rhs * live[None, None, :, None, None]
    scaling = precond[:, :, :, None, :]
    position = owner[neighbours[0, 0]]
    region = position // slots
    slot = position % slots
    step_lat = region // sectors - my_lat
    step_lon = (region % sectors - my_lon + 1) % sectors - 1
    local = ((step_lat + 1) * 3 + step_lon + 1) * slots + slot
    target = (jnp.arange(9 * slots)[:, None] == local.reshape(-1)[None, :]).astype(jnp.float32)
    weights = kriging[0, 0]
    blocks = factor[0, 0]
    solution = jnp.zeros_like(source)
    residual = source

    def residual_total(first, second):
        return lax.psum(inner(first, second), ("lat", "lon"))

    preconditioned = scaling * residual
    direction = preconditioned
    current = residual_total(residual, preconditioned)
    for step in range(ITERS):
        rounded = direction.astype(jnp.bfloat16)
        beside_all = with_halo(rounded, (("lat", 0), ("lon", 1)), 1)
        panel = beside_all.reshape(9 * slots, samples, width)[local]
        lifted = rounded[0, 0].astype(jnp.float32) - jnp.einsum(
            "knij,knsj->ksi", weights, panel, preferred_element_type=jnp.float32
        )
        lifted = lifted.astype(jnp.bfloat16)
        whitened = (
            jnp.einsum("kij,ksj->ksi", blocks, lifted, preferred_element_type=jnp.float32)
            * live[:, None, None]
        )
        whitened = whitened.astype(jnp.bfloat16)
        back = jnp.einsum("kji,ksj->ksi", blocks, whitened, preferred_element_type=jnp.float32)
        spread = -jnp.einsum(
            "knji,ksj->knsi", weights, back.astype(jnp.bfloat16), preferred_element_type=jnp.float32
        )
        placed = jnp.dot(
            target, spread.reshape(slots * links, samples * width), precision=lax.Precision.HIGHEST
        )
        placed = placed.reshape(3, 3, slots, samples, width)
        middle = placed[:, 1] + lon_back(placed[:, 2], 1) + lon_back(placed[:, 0], -1)
        total = middle[1] + lat_back(middle[2], 1) + lat_back(middle[0], -1)
        image = (back + total)[None, None] + nugget * direction
        alpha = current / lax.psum(inner(direction, image), ("lat", "lon"))
        solution = solution + alpha[:, None] * direction
        residual = residual - alpha[:, None] * image
        if step + 1 < ITERS:
            preconditioned = scaling * residual
            following = residual_total(residual, preconditioned)
            direction = preconditioned + (following / current)[:, None] * direction
            current = following
    return (solution, residual)


def solution(mesh):
    return jax.shard_map(
        body,
        mesh=mesh,
        in_specs=(
            P("lat", "lon", None, None, None),
            P("lat", "lon", None, None),
            P("lat", "lon", None, None, None),
            P("lat", "lon", None, None, None, None),
            P("lat", "lon", None, None),
            P(),
            P("lat", "lon"),
        ),
        out_specs=(P("lat", "lon", None, None, None), P("lat", "lon", None, None, None)),
        check_vma=False,
    )
```

profile of v0, /device:TPU:1, one launch (start us, length us, event | category | flops | bytes accessed | tf_op | source)
XLA Modules:
  0.0 421.8 jit_solution(18384698949551810775)
XLA Ops:
  3.3 6.9 %collective-permute-start.1 = (bf16[1,1,6,16,256]{4,3,2,1,0:T(8,128)(2,1)S(1)}, bf16[1,1,6,16,256]{4,3,2,1,0:T(8,128)(2,1)S(1)}, u32[]{:S(2)}, u32[]{:S(2)}) collective-permute-start(bf16[1,1,6,16,256]{4,3,2,1,0:T(8,128)(2,1)S(1)} %multiply_convert_fusion), channel_id=1, source_target_pairs={{64,0},{128,64},{192,128},{256,192},{320,256},{384,320},{448,384},... | collective-permute-start | bytes 147464 | tf_op jit(solution)/shard_map/ppermute | solution.py:33
  11.0 1.4 gather_fusion
  13.3 9.3 %collective-permute-start.3 = (bf16[3,1,6,16,256]{4,3,2,1,0:T(8,128)(2,1)S(1)}, bf16[3,1,6,16,256]{4,3,2,1,0:T(8,128)(2,1)S(1)}, u32[]{:S(2)}, u32[]{:S(2)}) collective-permute-start(bf16[3,1,6,16,256]{4,3,2,1,0:T(8,128)(2,1)S(1)} %pad_maximum_fusion.2), channel_id=1, source_target_pairs={{1,0},{2,1},{3,2},{4,3},{5,4},{6,5},{7,6},{8,7},{9,8},{10,9},{11,1... | collective-permute-start | bytes 442376 | tf_op jit(solution)/shard_map/ppermute | solution.py:33
  22.6 1.9 collective-permute-start.2
  24.7 7.1 %collective-permute-done.2 = bf16[3,1,6,16,256]{4,3,2,1,0:T(8,128)(2,1)S(1)} collective-permute-done((bf16[3,1,6,16,256]{4,3,2,1,0:T(8,128)(2,1)S(1)}, bf16[3,1,6,16,256]{4,3,2,1,0:T(8,128)(2,1)S(1)}, u32[]{:S(2)}, u32[]{:S(2)}) %collective-permute-start.2) | collective-permute-done | bytes 147488 | tf_op jit(solution)/shard_map/ppermute | solution.py:30
  32.6 1.6 gather_fusion.1
  35.2 1.8 fusion.35
  38.7 1.9 collective-permute-start.4
  40.7 6.7 %collective-permute-start.5 = (bf16[3,6,16,256]{3,2,1,0:T(8,128)(2,1)S(1)}, bf16[3,6,16,256]{3,2,1,0:T(8,128)(2,1)S(1)}, u32[]{:S(2)}, u32[]{:S(2)}) collective-permute-start(bf16[3,6,16,256]{3,2,1,0:T(8,128)(2,1)S(1)} %get-tuple-element.21), channel_id=1, source_target_pairs={{1,0},{2,1},{3,2},{4,3},{5,4},{6,5},{7,6},{8,7},{9,8},{10,9},{11,1... | collective-permute-start | bytes 442376 | tf_op jit(solution)/shard_map/ppermute | solution.py:15
  48.0 1.5 collective-permute-done.5
  49.5 6.7 %collective-permute-start.6 = (bf16[6,16,256]{2,1,0:T(8,128)(2,1)S(1)}, bf16[6,16,256]{2,1,0:T(8,128)(2,1)S(1)}, u32[]{:S(2)}, u32[]{:S(2)}) collective-permute-start(bf16[6,16,256]{2,1,0:T(8,128)(2,1)S(1)} %get-tuple-element.26), channel_id=1, source_target_pairs={{0,64},{64,128},{128,192},{192,256},{256,320},{320,384},{384,448},... | collective-permute-start | bytes 147464 | tf_op jit(solution)/shard_map/ppermute | solution.py:21
  56.3 1.9 collective-permute-start.7
  58.2 3.5 collective-permute-done.7
  61.9 102.7 %all-reduce = (f32[16]{0:T(128)S(1)}, f32[16]{0:T(128)S(1)}) all-reduce(f32[16]{0:T(128)S(1)} %get-tuple-element.3, f32[16]{0:T(128)S(1)} %get-tuple-element.2), channel_id=1, replica_groups=mesh['lat'=8,'lon'=64] {'lat','lon'}, use_global_device_ids=true, to_apply=%region_1.2 | all-reduce | flops 32 | bytes 256 | tf_op jit(solution)/shard_map/psum | solution.py:74
  165.1 1.6 fusion.51
  166.7 99.2 %psum.30 = f32[16]{0:T(128)S(1)} all-reduce(f32[16]{0:T(128)} %get-tuple-element.10), channel_id=1, replica_groups=mesh['lat'=8,'lon'=64] {'lat','lon'}, use_global_device_ids=true, to_apply=%region_5.6 | all-reduce | flops 16 | bytes 128 | tf_op jit(solution)/shard_map/psum | solution.py:74
  268.5 1.1 collective-permute-start.8
  269.6 1.8 collective-permute-done.9
  271.4 5.3 %collective-permute-start.11 = (bf16[3,1,6,16,256]{4,3,2,1,0:T(8,128)(2,1)S(1)}, bf16[3,1,6,16,256]{4,3,2,1,0:T(8,128)(2,1)S(1)}, u32[]{:S(2)}, u32[]{:S(2)}) collective-permute-start(bf16[3,1,6,16,256]{4,3,2,1,0:T(8,128)(2,1)S(1)} %pad_maximum_fusion.3), channel_id=1, source_target_pairs={{1,0},{2,1},{3,2},{4,3},{5,4},{6,5},{7,6},{8,7},{9,8},{10,9},{11,1... | collective-permute-start | bytes 442376 | tf_op jit(solution)/shard_map/ppermute | solution.py:33
  276.7 1.9 collective-permute-start.10
  278.8 7.1 %collective-permute-done.10 = bf16[3,1,6,16,256]{4,3,2,1,0:T(8,128)(2,1)S(1)} collective-permute-done((bf16[3,1,6,16,256]{4,3,2,1,0:T(8,128)(2,1)S(1)}, bf16[3,1,6,16,256]{4,3,2,1,0:T(8,128)(2,1)S(1)}, u32[]{:S(2)}, u32[]{:S(2)}) %collective-permute-start.10) | collective-permute-done | bytes 147488 | tf_op jit(solution)/shard_map/ppermute | solution.py:30
  286.7 1.7 gather_fusion.2
  288.4 2.4 fusion.29
  290.8 1.8 fusion.34
  294.4 1.9 collective-permute-start.12
  296.3 6.7 %collective-permute-start.13 = (bf16[3,6,16,256]{3,2,1,0:T(8,128)(2,1)S(1)}, bf16[3,6,16,256]{3,2,1,0:T(8,128)(2,1)S(1)}, u32[]{:S(2)}, u32[]{:S(2)}) collective-permute-start(bf16[3,6,16,256]{3,2,1,0:T(8,128)(2,1)S(1)} %get-tuple-element.19), channel_id=1, source_target_pairs={{1,0},{2,1},{3,2},{4,3},{5,4},{6,5},{7,6},{8,7},{9,8},{10,9},{11,1... | collective-permute-start | bytes 442376 | tf_op jit(solution)/shard_map/ppermute | solution.py:15
  303.6 1.5 collective-permute-done.13
  305.2 6.2 %collective-permute-start.14 = (bf16[6,16,256]{2,1,0:T(8,128)(2,1)S(1)}, bf16[6,16,256]{2,1,0:T(8,128)(2,1)S(1)}, u32[]{:S(2)}, u32[]{:S(2)}) collective-permute-start(bf16[6,16,256]{2,1,0:T(8,128)(2,1)S(1)} %get-tuple-element.24), channel_id=1, source_target_pairs={{0,64},{64,128},{128,192},{192,256},{256,320},{320,384},{384,448},... | collective-permute-start | bytes 147464 | tf_op jit(solution)/shard_map/ppermute | solution.py:21
  311.4 1.9 collective-permute-start.15
  313.4 3.5 collective-permute-done.15
  317.6 101.8 %psum.31 = f32[16]{0:T(128)} all-reduce(f32[16]{0:T(128)} %multiply_reduce_fusion), channel_id=1, replica_groups=mesh['lat'=8,'lon'=64] {'lat','lon'}, use_global_device_ids=true, to_apply=%region_7.8 | all-reduce | flops 16 | bytes 128 | tf_op jit(solution)/shard_map/psum | solution.py:103
  420.1 1.7 multiply_subtract_fusion
  (90 shorter events, 15.9 us)
Async XLA Ops:
  0.6 33.6 %copy-start = (bf16[1,1,6,4,256,256]{5,4,3,2,1,0:T(8,128)(2,1)S(1)}, bf16[1,1,6,4,256,256]{5,4,3,2,1,0:T(8,128)(2,1)}, u32[]{:S(2)}) copy-start(bf16[1,1,6,4,256,256]{5,4,3,2,1,0:T(8,128)(2,1)} %param.10) | copy-start | bytes 9437188
  1.5 33.7 %copy-start.6 = (f32[6]{0:T(128)}, f32[6]{0:T(128)S(1)}, u32[]{:S(2)}) copy-start(f32[6]{0:T(128)S(1)} %compare_convert_fusion) | copy-start | bytes 76
  3.3 10.0 %collective-permute-start.1 = (bf16[1,1,6,16,256]{4,3,2,1,0:T(8,128)(2,1)S(1)}, bf16[1,1,6,16,256]{4,3,2,1,0:T(8,128)(2,1)S(1)}, u32[]{:S(2)}, u32[]{:S(2)}) collective-permute-start(bf16[1,1,6,16,256]{4,3,2,1,0:T(8,128)(2,1)S(1)} %multiply_convert_fusion), channel_id=1, source_target_pairs={{64,0},{128,64},{192,128},{256,192},{320,256},{384,320},{448,384},... | collective-permute-start | bytes 147464 | tf_op jit(solution)/shard_map/ppermute | solution.py:33
  10.2 3.1 collective-permute-start
  12.7 24.8 %copy-start.10 = (s32[24]{0:T(128)}, s32[24]{0:T(128)S(1)}, u32[]{:S(2)}) copy-start(s32[24]{0:T(128)S(1)} %get-tuple-element.16) | copy-start | bytes 292
  13.3 11.4 %collective-permute-start.3 = (bf16[3,1,6,16,256]{4,3,2,1,0:T(8,128)(2,1)S(1)}, bf16[3,1,6,16,256]{4,3,2,1,0:T(8,128)(2,1)S(1)}, u32[]{:S(2)}, u32[]{:S(2)}) collective-permute-start(bf16[3,1,6,16,256]{4,3,2,1,0:T(8,128)(2,1)S(1)} %pad_maximum_fusion.2), channel_id=1, source_target_pairs={{1,0},{2,1},{3,2},{4,3},{5,4},{6,5},{7,6},{8,7},{9,8},{10,9},{11,1... | collective-permute-start | bytes 442376 | tf_op jit(solution)/shard_map/ppermute | solution.py:33
  22.6 9.2 %collective-permute-start.2 = (bf16[3,1,6,16,256]{4,3,2,1,0:T(8,128)(2,1)S(1)}, bf16[3,1,6,16,256]{4,3,2,1,0:T(8,128)(2,1)S(1)}, u32[]{:S(2)}, u32[]{:S(2)}) collective-permute-start(bf16[3,1,6,16,256]{4,3,2,1,0:T(8,128)(2,1)S(1)} %pad_maximum_fusion.2), channel_id=1, source_target_pairs={{0,1},{1,2},{2,3},{3,4},{4,5},{5,6},{6,7},{7,8},{8,9},{9,10},{10,1... | collective-permute-start | bytes 442376 | tf_op jit(solution)/shard_map/ppermute | solution.py:30
  24.6 12.4 %copy-start.5 = (s32[1024]{0:T(1024)}, s32[1024]{0:T(1024)S(1)}, u32[]{:S(2)}) copy-start(s32[1024]{0:T(1024)S(1)} %pad_clamp_fusion) | copy-start | bytes 12292
  37.5 24.2 %copy-start.1 = (f32[1,1,6,16,256]{4,3,2,1,0:T(8,128)S(1)}, f32[1,1,6,16,256]{4,3,2,1,0:T(8,128)}, u32[]{:S(2)}) copy-start(f32[1,1,6,16,256]{4,3,2,1,0:T(8,128)} %param.7) | copy-start | bytes 294916
  37.5 24.2 %copy-start.7 = (f32[6]{0:T(128)S(1)}, f32[6]{0:T(128)}, u32[]{:S(2)}) copy-start(f32[6]{0:T(128)} %copy-done.6) | copy-start | bytes 76
  38.7 9.2 %collective-permute-start.4 = (bf16[3,6,16,256]{3,2,1,0:T(8,128)(2,1)S(1)}, bf16[3,6,16,256]{3,2,1,0:T(8,128)(2,1)S(1)}, u32[]{:S(2)}, u32[]{:S(2)}) collective-permute-start(bf16[3,6,16,256]{3,2,1,0:T(8,128)(2,1)S(1)} %get-tuple-element.20), channel_id=1, source_target_pairs={{63,0},{0,1},{1,2},{2,3},{3,4},{4,5},{5,6},{6,7},{7,8},{8,9},{9,10... | collective-permute-start | bytes 442376 | tf_op jit(solution)/shard_map/ppermute | solution.py:15
  40.7 8.8 %collective-permute-start.5 = (bf16[3,6,16,256]{3,2,1,0:T(8,128)(2,1)S(1)}, bf16[3,6,16,256]{3,2,1,0:T(8,128)(2,1)S(1)}, u32[]{:S(2)}, u32[]{:S(2)}) collective-permute-start(bf16[3,6,16,256]{3,2,1,0:T(8,128)(2,1)S(1)} %get-tuple-element.21), channel_id=1, source_target_pairs={{1,0},{2,1},{3,2},{4,3},{5,4},{6,5},{7,6},{8,7},{9,8},{10,9},{11,1... | collective-permute-start | bytes 442376 | tf_op jit(solution)/shard_map/ppermute | solution.py:15
  49.5 12.2 %copy-start.2 = (f32[3,6,16,256]{3,2,1,0:T(8,128)}, f32[3,6,16,256]{3,2,1,0:T(8,128)S(1)}, u32[]{:S(2)}) copy-start(f32[3,6,16,256]{3,2,1,0:T(8,128)S(1)} %get-tuple-element.13) | copy-start | bytes 884740
  49.5 8.6 %collective-permute-start.6 = (bf16[6,16,256]{2,1,0:T(8,128)(2,1)S(1)}, bf16[6,16,256]{2,1,0:T(8,128)(2,1)S(1)}, u32[]{:S(2)}, u32[]{:S(2)}) collective-permute-start(bf16[6,16,256]{2,1,0:T(8,128)(2,1)S(1)} %get-tuple-element.26), channel_id=1, source_target_pairs={{0,64},{64,128},{128,192},{192,256},{256,320},{320,384},{384,448},... | collective-permute-start | bytes 147464 | tf_op jit(solution)/shard_map/ppermute | solution.py:21
  56.3 5.4 %collective-permute-start.7 = (bf16[6,16,256]{2,1,0:T(8,128)(2,1)S(1)}, bf16[6,16,256]{2,1,0:T(8,128)(2,1)S(1)}, u32[]{:S(2)}, u32[]{:S(2)}) collective-permute-start(bf16[6,16,256]{2,1,0:T(8,128)(2,1)S(1)} %get-tuple-element.27), channel_id=1, source_target_pairs={{64,0},{128,64},{192,128},{256,192},{320,256},{384,320},{448,384},... | collective-permute-start | bytes 147464 | tf_op jit(solution)/shard_map/ppermute | solution.py:21
  165.1 1.6 copy-start.15
  266.0 0.6 copy-start.16
  267.8 18.9 %copy-start.4 = (bf16[1,1,6,16,256]{4,3,2,1,0:T(8,128)(2,1)}, bf16[1,1,6,16,256]{4,3,2,1,0:T(8,128)(2,1)S(1)}, u32[]{:S(2)}) copy-start(bf16[1,1,6,16,256]{4,3,2,1,0:T(8,128)(2,1)S(1)} %fusion.93) | copy-start | bytes 147460
  267.9 3.5 collective-permute-start.9
  268.5 2.8 collective-permute-start.8
  271.4 7.4 %collective-permute-start.11 = (bf16[3,1,6,16,256]{4,3,2,1,0:T(8,128)(2,1)S(1)}, bf16[3,1,6,16,256]{4,3,2,1,0:T(8,128)(2,1)S(1)}, u32[]{:S(2)}, u32[]{:S(2)}) collective-permute-start(bf16[3,1,6,16,256]{4,3,2,1,0:T(8,128)(2,1)S(1)} %pad_maximum_fusion.3), channel_id=1, source_target_pairs={{1,0},{2,1},{3,2},{4,3},{5,4},{6,5},{7,6},{8,7},{9,8},{10,9},{11,1... | collective-permute-start | bytes 442376 | tf_op jit(solution)/shard_map/ppermute | solution.py:33
  276.7 9.2 %collective-permute-start.10 = (bf16[3,1,6,16,256]{4,3,2,1,0:T(8,128)(2,1)S(1)}, bf16[3,1,6,16,256]{4,3,2,1,0:T(8,128)(2,1)S(1)}, u32[]{:S(2)}, u32[]{:S(2)}) collective-permute-start(bf16[3,1,6,16,256]{4,3,2,1,0:T(8,128)(2,1)S(1)} %pad_maximum_fusion.3), channel_id=1, source_target_pairs={{0,1},{1,2},{2,3},{3,4},{4,5},{5,6},{6,7},{7,8},{8,9},{9,10},{10,1... | collective-permute-start | bytes 442376 | tf_op jit(solution)/shard_map/ppermute | solution.py:30
  290.8 2.4 copy-start.11
  293.1 23.7 %copy-start.8 = (f32[6]{0:T(128)S(1)}, f32[6]{0:T(128)}, u32[]{:S(2)}) copy-start(f32[6]{0:T(128)} %copy-done.6) | copy-start | bytes 76
  293.1 23.7 %copy-start.13 = (f32[16]{0:T(128)S(1)}, f32[16]{0:T(128)}, u32[]{:S(2)}) copy-start(f32[16]{0:T(128)} %copy-done.12) | copy-start | bytes 196
  294.1 126.0 %copy-start.9 = (f32[6]{0:T(128)S(1)}, f32[6]{0:T(128)}, u32[]{:S(2)}) copy-start(f32[6]{0:T(128)} %copy-done.6) | copy-start | bytes 76
  294.1 126.0 %copy-start.14 = (f32[16]{0:T(128)S(1)}, f32[16]{0:T(128)}, u32[]{:S(2)}) copy-start(f32[16]{0:T(128)} %copy-done.12) | copy-start | bytes 196
  294.4 9.2 %collective-permute-start.12 = (bf16[3,6,16,256]{3,2,1,0:T(8,128)(2,1)S(1)}, bf16[3,6,16,256]{3,2,1,0:T(8,128)(2,1)S(1)}, u32[]{:S(2)}, u32[]{:S(2)}) collective-permute-start(bf16[3,6,16,256]{3,2,1,0:T(8,128)(2,1)S(1)} %get-tuple-element.18), channel_id=1, source_target_pairs={{63,0},{0,1},{1,2},{2,3},{3,4},{4,5},{5,6},{6,7},{7,8},{8,9},{9,10... | collective-permute-start | bytes 442376 | tf_op jit(solution)/shard_map/ppermute | solution.py:15
  296.3 8.8 %collective-permute-start.13 = (bf16[3,6,16,256]{3,2,1,0:T(8,128)(2,1)S(1)}, bf16[3,6,16,256]{3,2,1,0:T(8,128)(2,1)S(1)}, u32[]{:S(2)}, u32[]{:S(2)}) collective-permute-start(bf16[3,6,16,256]{3,2,1,0:T(8,128)(2,1)S(1)} %get-tuple-element.19), channel_id=1, source_target_pairs={{1,0},{2,1},{3,2},{4,3},{5,4},{6,5},{7,6},{8,7},{9,8},{10,9},{11,1... | collective-permute-start | bytes 442376 | tf_op jit(solution)/shard_map/ppermute | solution.py:15
  305.2 11.7 %copy-start.3 = (f32[3,6,16,256]{3,2,1,0:T(8,128)}, f32[3,6,16,256]{3,2,1,0:T(8,128)S(1)}, u32[]{:S(2)}) copy-start(f32[3,6,16,256]{3,2,1,0:T(8,128)S(1)} %get-tuple-element.7) | copy-start | bytes 884740
  305.2 8.2 %collective-permute-start.14 = (bf16[6,16,256]{2,1,0:T(8,128)(2,1)S(1)}, bf16[6,16,256]{2,1,0:T(8,128)(2,1)S(1)}, u32[]{:S(2)}, u32[]{:S(2)}) collective-permute-start(bf16[6,16,256]{2,1,0:T(8,128)(2,1)S(1)} %get-tuple-element.24), channel_id=1, source_target_pairs={{0,64},{64,128},{128,192},{192,256},{256,320},{320,384},{384,448},... | collective-permute-start | bytes 147464 | tf_op jit(solution)/shard_map/ppermute | solution.py:21
  311.4 5.4 %collective-permute-start.15 = (bf16[6,16,256]{2,1,0:T(8,128)(2,1)S(1)}, bf16[6,16,256]{2,1,0:T(8,128)(2,1)S(1)}, u32[]{:S(2)}, u32[]{:S(2)}) collective-permute-start(bf16[6,16,256]{2,1,0:T(8,128)(2,1)S(1)} %get-tuple-element.25), channel_id=1, source_target_pairs={{64,0},{128,64},{192,128},{256,192},{320,256},{384,320},{448,384},... | collective-permute-start | bytes 147464 | tf_op jit(solution)/shard_map/ppermute | solution.py:21
  (2 other events, 1.1 us)
where the time goes:
time: 423 us; the launch traced here: 422 us
  blocking collectives  304 us (72%)
  starting transfers between devices  61.1 us (14%)
  waiting for transfers between devices  27.4 us (6%)
  other arithmetic  10.4 us (2%)
  matrix products  9.73 us (2%)
  local copies, waits for them, and re-layouts  7.63 us (2%)
    psum x2, blocking collectives, residual_total(): return lax.psum(inner(first, second), ('lat', 'lon'))  202 us
    psum x1, blocking collectives, body(): alpha = current / lax.psum(inner(direction, image), ('lat', 'lon'))  102 us
    ppermute x4, starting transfers between devices, with_halo(): lax.ppermute(lax.slice_in_dim(block, 0, width, axis=dim), axis, backward)  22.2 us
    ppermute x4, starting transfers between devices, from_behind(): return lax.ppermute(block, axis, route)  17.2 us
    ppermute x4, starting transfers between devices, from_behind_2(): lax.ppermute(value, axis, [(source, source + steps) for source in range(l...  16.8 us
    ppermute x4, waiting for transfers between devices, with_halo(): lax.ppermute(lax.slice_in_dim(block, block.shape[dim] - width, None, axis...  14.3 us
  transfers between devices with their start and end apart: 16, of which 11 were waited for; matrix products, arithmetic and copies ran while one was open for 1% of the time, Pallas kernels for 0%

commit v1 on v0

v1 whole, which is shorter than its diff:
```python
import functools

import jax
import jax.numpy as jnp
from jax import lax
from jax.experimental import pallas as pl
from jax.experimental.pallas import tpu as pltpu
from jax.sharding import PartitionSpec as P

ROW = 16
LANES = 128
SMALL = 2.0**-75
NEAR = (0, 1, 2, 3, 5, 6, 7, 8)


def dot(a, b):
    return lax.dot_general(a, b, (((1,), (0,)), ((), ())), preferred_element_type=jnp.float32)


def dot_t(a, b):
    return lax.dot_general(a, b, (((1,), (1,)), ((), ())), preferred_element_type=jnp.float32)


def kernel(
    sizes,
    rhs_hbm, pre_hbm, fac_hbm, kri_hbm, near_ref, owner_ref, count_ref,
    sol_ref, res_ref,
    rhs, pre, fac, kri, lifted, halo, spread, select, out, arrive, row_sum, col_sum,
    load_sem, halo_send, halo_recv, back_send, back_recv, row_send, row_recv, col_send, col_recv,
):
    lats, lons, row = sizes
    slots, samples, width = rhs.shape
    links = kri.shape[1]
    high = slots * samples
    cols = lats * (lons // row)
    lat, lon = lax.axis_index("lat"), lax.axis_index("lon")
    ring, place = lax.rem(lon, row), lax.div(lon, row)
    wide = lons // row
    block = lat * wide + place

    loads = [
        pltpu.make_async_copy(rhs_hbm, rhs, load_sem.at[0]),
        pltpu.make_async_copy(pre_hbm, pre, load_sem.at[1]),
        pltpu.make_async_copy(kri_hbm, kri, load_sem.at[2]),
        pltpu.make_async_copy(fac_hbm, fac, load_sem.at[3]),
    ]
    for load in loads:
        load.start()

    def beside(r):
        up, side = r // 3 - 1, r % 3 - 1
        there = lat + up
        valid = jnp.logical_and(there >= 0, there < lats)
        return valid, (there, lax.rem(lon + side + lons, lons))

    def row_mate(step):
        return (lat, place * row + lax.rem(ring + step, row))

    def col_mate(step):
        other = lax.rem(block + step, cols)
        return (lax.div(other, wide), lax.rem(other, wide) * row + ring)

    def far_first(n):
        return sorted(range(1, n), key=lambda o: -min(o, n - o))

    barrier = pltpu.get_barrier_semaphore()

    def greet(device):
        pl.semaphore_signal(barrier, inc=1, device_id=device, device_id_type=pl.DeviceIdType.MESH)

    for step in far_first(row):
        greet(row_mate(step))
    for step in far_first(cols):
        greet(col_mate(step))
    for r in NEAR:
        valid, device = beside(r)
        pl.when(valid)(functools.partial(greet, device))
    edge = jnp.logical_or(lat == 0, lat == lats - 1)
    around = jnp.where(edge, 5, 8)

    wanted = []
    for b in range(slots):
        for m in range(links):
            position = owner_ref[near_ref[b, m]]
            region = position // slots
            slot = position - region * slots
            region_lat = region // lons
            up = region_lat - lat
            side = lax.rem(region - region_lat * lons - lon + 1 + lons, lons)
            index = ((up + 1) * 3 + side) * slots + slot
            wanted.append(jnp.clip(index, 0, 9 * slots - 1))
    live = [jnp.where(b < count_ref[0, 0], 1.0, 0.0).astype(jnp.float32) for b in range(slots)]

    depth = slots * links * samples
    lane = lax.broadcasted_iota(jnp.int32, (1, depth), 1)
    link, sample = lane // samples, lane % samples
    goal = sample
    for i, w in enumerate(wanted):
        goal = goal + jnp.where(link == i, w * samples, 0)
    for r in range(9):
        rows = lax.broadcasted_iota(jnp.int32, (high, depth), 0) + r * high
        select[r] = jnp.where(rows == goal, 1.0, 0.0).astype(jnp.bfloat16)

    @pl.when(lat == 0)
    def _():
        for k in range(2):
            arrive[k, 0:3] = jnp.zeros((3, high, width), jnp.bfloat16)
            halo[k, 0 : 3 * slots] = jnp.zeros((3 * slots, samples, width), jnp.bfloat16)

    @pl.when(lat == lats - 1)
    def _():
        for k in range(2):
            arrive[k, 6:9] = jnp.zeros((3, high, width), jnp.bfloat16)
            halo[k, 6 * slots : 9 * slots] = jnp.zeros((3 * slots, samples, width), jnp.bfloat16)

    def remote(source, target, send, recv, device):
        return pltpu.make_async_remote_copy(
            src_ref=source, dst_ref=target, send_sem=send, recv_sem=recv,
            device_id=device, device_id_type=pl.DeviceIdType.MESH,
        )

    def halo_copy(k, r):
        valid, device = beside(r)
        copy = remote(
            halo.at[k, pl.ds(4 * slots, slots)], halo.at[k, pl.ds((8 - r) * slots, slots)],
            halo_send.at[k, r], halo_recv.at[k, 8 - r], device,
        )
        return valid, copy

    def halo_arrival(k, r):
        valid, device = beside(r)
        here = halo.at[k, pl.ds(r * slots, slots)]
        return valid, remote(here, here, halo_send.at[k, r], halo_recv.at[k, r], device)

    def back_copy(k, r):
        valid, device = beside(r)
        copy = remote(
            out.at[k, r], arrive.at[k, 8 - r], back_send.at[k, r], back_recv.at[k, 8 - r], device
        )
        return valid, copy

    def back_arrival(k, r):
        valid, device = beside(r)
        here = arrive.at[k, r]
        return valid, remote(here, here, back_send.at[k, r], back_recv.at[k, r], device)

    def send_field(k, parts):
        for b in range(slots):
            halo[k, 4 * slots + b] = parts[b].astype(jnp.bfloat16)
        for r in NEAR:
            valid, copy = halo_copy(k, r)
            pl.when(valid)(copy.start)

    def gather(k):
        for r in NEAR:
            valid, copy = halo_arrival(k, r)
            pl.when(valid)(copy.wait_recv)
        parts = []
        for b in range(slots):
            total = jnp.zeros((samples, width), jnp.float32)
            for m in range(links):
                total = total + dot_t(halo[k, wanted[b * links + m]], kri[b, m])
            parts.append(total)
        return parts

    def whiten(parts):
        return [dot_t(parts[b].astype(jnp.bfloat16), fac[b]) * live[b] for b in range(slots)]

    def send_back(k, white):
        backs = []
        for b in range(slots):
            back = dot(white[b].astype(jnp.bfloat16), fac[b])
            backs.append(back)
            low = back.astype(jnp.bfloat16)
            for m in range(links):
                i = b * links + m
                spread[i * samples : (i + 1) * samples] = (-dot(low, kri[b, m])).astype(jnp.bfloat16)
        terms = spread[...]
        for r in NEAR:
            out[k, r] = dot(select[r], terms).astype(jnp.bfloat16)
            valid, copy = back_copy(k, r)
            pl.when(valid)(copy.start)
        mine = dot(select[4], terms)
        return [backs[b] + mine[b * samples : (b + 1) * samples] for b in range(slots)]

    def take_back(k, parts):
        for r in NEAR:
            valid, copy = back_arrival(k, r)
            pl.when(valid)(copy.wait_recv)
        total = list(parts)
        for r in NEAR:
            for b in range(slots):
                piece = arrive[k, r, b * samples : (b + 1) * samples]
                total[b] = total[b] + piece.astype(jnp.float32)
        return total

    diagonal = lax.broadcasted_iota(jnp.int32, (samples, LANES), 1) - lax.broadcasted_iota(
        jnp.int32, (samples, LANES), 0
    )

    def inner(first, second):
        total = first[0] * second[0]
        for b in range(1, slots):
            total = total + first[b] * second[b]
        return jnp.sum(total, axis=1, keepdims=True)

    def row_copy(k, step):
        here = row_sum.at[k, ring]
        return remote(here, here, row_send.at[k], row_recv.at[k], row_mate(step))

    def col_copy(k, step):
        here = col_sum.at[k, block]
        return remote(here, here, col_send.at[k], col_recv.at[k], col_mate(step))

    def sum_first(k, columns):
        packed = jnp.zeros((samples, LANES), jnp.float32)
        for i, column in enumerate(columns):
            packed = packed + jnp.where(diagonal == i * samples, column, 0.0)
        row_sum[k, ring] = jnp.sum(packed, axis=0, keepdims=True)
        for step in far_first(row):
            row_copy(k, step).start()

    def sum_second(k):
        many = row_sum.at[k, pl.ds(0, row - 1)]
        remote(many, many, row_send.at[k], row_recv.at[k], row_mate(1)).wait_recv()
        col_sum[k, block] = jnp.sum(row_sum[k], axis=0)
        for step in far_first(cols):
            col_copy(k, step).start()

    def sum_last(k, n):
        many = col_sum.at[k, pl.ds(0, cols - 1)]
        remote(many, many, col_send.at[k], col_recv.at[k], col_mate(1)).wait_recv()
        total = jnp.broadcast_to(jnp.sum(col_sum[k], axis=0), (samples, LANES))
        return [
            jnp.sum(jnp.where(diagonal == i * samples, total, 0.0), axis=1, keepdims=True)
            for i in range(n)
        ]

    def sums_sent(k):
        many = row_sum.at[k, pl.ds(0, row - 1)]
        remote(many, many, row_send.at[k], row_recv.at[k], row_mate(1)).wait_send()
        many = col_sum.at[k, pl.ds(0, cols - 1)]
        remote(many, many, col_send.at[k], col_recv.at[k], col_mate(1)).wait_send()

    loads[0].wait()
    loads[1].wait()
    each = range(slots)
    source = [rhs[b] * live[b] for b in each]
    scale = [pre[b : b + 1] for b in each]
    first = [scale[b] * source[b] for b in each]
    pl.semaphore_wait(barrier, row - 1 + cols - 1 + around)
    send_field(0, first)
    loads[2].wait()
    loads[3].wait()

    away = gather(0)
    for b in each:
        lifted[b] = first[b].astype(jnp.bfloat16).astype(jnp.float32) - away[b]
    image = send_back(0, whiten([lifted[b] for b in each]))
    image = take_back(0, image)
    image = [image[b] + first[b] for b in each]

    scaled = [scale[b] * image[b] for b in each]
    less = [SMALL * image[b] for b in each]
    columns = [
        inner(source, first),
        inner(first, image),
        inner(image, scaled),
        inner(less, [SMALL * scaled[b] for b in each]),
    ]
    sum_first(0, columns)
    send_field(1, scaled)
    sum_second(0)
    away = gather(1)
    current, slope, bend, bend_less = sum_last(0, 4)
    alpha = current / slope
    more = alpha * (1.0 / SMALL)
    square = jnp.where(bend < 3e38, (alpha * bend) * alpha, (more * bend_less) * more)
    following = current - 2.0 * alpha * slope + square
    beta = following / current
    second = [(first[b] - alpha * scaled[b]) + beta * first[b] for b in each]
    parts = [
        (1.0 + beta) * lifted[b] - alpha * (scaled[b].astype(jnp.bfloat16).astype(jnp.float32) - away[b])
        for b in each
    ]
    white = whiten(parts)
    sum_first(1, [inner(white, white) + inner(second, second)])
    turned = send_back(1, white)
    residual = [source[b] - alpha * image[b] for b in each]
    sum_second(1)
    turned = take_back(1, turned)
    [slope] = sum_last(1, 1)
    step_size = following / slope
    for b in each:
        sol_ref[b] = alpha * first[b] + step_size * second[b]
        res_ref[b] = residual[b] - step_size * (turned[b] + second[b])

    for k in range(2):
        for r in NEAR:
            valid, copy = halo_copy(k, r)
            pl.when(valid)(copy.wait_send)
            valid, copy = back_copy(k, r)
            pl.when(valid)(copy.wait_send)
        sums_sent(k)


def body(row, rhs, precond, factor, kriging, neighbours, owner, counts):
    slots, links, width = kriging.shape[2], kriging.shape[3], kriging.shape[4]
    samples = rhs.shape[3]
    lats, lons = lax.axis_size("lat"), lax.axis_size("lon")
    cols = lats * (lons // row)
    high = slots * samples
    field = jax.ShapeDtypeStruct((slots, samples, width), jnp.float32)
    anywhere = pl.BlockSpec(memory_space=pl.ANY)
    scalars = pl.BlockSpec(memory_space=pltpu.SMEM)
    vmem = pl.BlockSpec(memory_space=pltpu.VMEM)
    solved, left = pl.pallas_call(
        functools.partial(kernel, (lats, lons, row)),
        out_shape=(field, field),
        in_specs=[anywhere] * 4 + [scalars] * 3,
        out_specs=(vmem, vmem),
        scratch_shapes=[
            pltpu.VMEM((slots, samples, width), jnp.float32),
            pltpu.VMEM((slots, width), jnp.float32),
            pltpu.VMEM((slots, width, width), jnp.bfloat16),
            pltpu.VMEM((slots, links, width, width), jnp.bfloat16),
            pltpu.VMEM((slots, samples, width), jnp.float32),
            pltpu.VMEM((2, 9 * slots, samples, width), jnp.bfloat16),
            pltpu.VMEM((slots * links * samples, width), jnp.bfloat16),
            pltpu.VMEM((9, high, slots * links * samples), jnp.bfloat16),
            pltpu.VMEM((2, 9, high, width), jnp.bfloat16),
            pltpu.VMEM((2, 9, high, width), jnp.bfloat16),
            pltpu.VMEM((2, row, 1, LANES), jnp.float32),
            pltpu.VMEM((2, cols, 1, LANES), jnp.float32),
            pltpu.SemaphoreType.DMA((4,)),
            pltpu.SemaphoreType.DMA((2, 9)),
            pltpu.SemaphoreType.DMA((2, 9)),
            pltpu.SemaphoreType.DMA((2, 9)),
            pltpu.SemaphoreType.DMA((2, 9)),
            pltpu.SemaphoreType.DMA((2,)),
            pltpu.SemaphoreType.DMA((2,)),
            pltpu.SemaphoreType.DMA((2,)),
            pltpu.SemaphoreType.DMA((2,)),
        ],
        compiler_params=pltpu.CompilerParams(
            collective_id=0, has_side_effects=True, vmem_limit_bytes=32 * 2**20
        ),
    )(rhs[0, 0], precond[0, 0], factor[0, 0], kriging[0, 0], neighbours[0, 0], owner, counts)
    return solved[None, None], left[None, None]


def solution(mesh):
    lons = mesh.shape["lon"]
    row = ROW if lons % ROW == 0 else 2
    return jax.shard_map(
        functools.partial(body, row),
        mesh=mesh,
        in_specs=(
            P("lat", "lon", None, None, None),
            P("lat", "lon", None, None),
            P("lat", "lon", None, None, None),
            P("lat", "lon", None, None, None, None),
            P("lat", "lon", None, None),
            P(),
            P("lat", "lon"),
        ),
        out_specs=(P("lat", "lon", None, None, None), P("lat", "lon", None, None, None)),
        check_vma=False,
    )
```

time: 423 us -> 66.7 us (0.16)
  blocking collectives: 304 us -> 0 us
  starting transfers between devices: 61.1 us -> 0 us
  Pallas kernels: 0 us -> 57.7 us
  waiting for transfers between devices: 27.4 us -> 0 us
  other arithmetic: 10.4 us -> 0 us
  matrix products: 9.73 us -> 0 us
    psum x3 -> x0, blocking collectives: 304 us -> none  [the longest x2 202 us: residual_total(): return lax.psum(inner(first, second), ('lat', 'lon'))]
    ppermute x16 -> x0, starting transfers between devices: 61.1 us -> none  [the longest x4 22.2 us: with_halo(): lax.ppermute(lax.slice_in_dim(block, 0, width, axis=dim), axis, backward)]
    pallas_call x0 -> x1, Pallas kernels: none -> 57.7 us  [body(): pl.pallas_call(functools.partial(kernel, (lats, lons, row)), out_shape=(f...]
    ppermute x16 -> x0, waiting for transfers between devices: 27.4 us -> none  [the longest x4 14.3 us: with_halo(): lax.ppermute(lax.slice_in_dim(block, block.shape[dim] - width, None, axis...]
    dot_general x8 -> x0, matrix products: 9.73 us -> none  [the longest x2 3.64 us: body(): jnp.einsum('kji,ksj->ksi', blocks, whitened, preferred_element_type=jnp.f...]
    gather x3 -> x0, local copies, waits for them, and re-layouts: 4.68 us -> none  [the longest x2 3.27 us: body(): panel = beside_all.reshape(9 * slots, samples, width)[local]]
    unnamed x37 -> x11, local copies, waits for them, and re-layouts: 2 us -> 6.6 us
  transfers between devices with their start and end apart: 16 -> 0, of which waited for: 11 -> 0; matrix products, arithmetic and copies ran while one was open for 1% -> 0% of each run, Pallas kernels for 0% -> 0%
where the time goes in v1:
time: 66.7 us; the launch traced here: 66.4 us
  Pallas kernels  57.7 us (87%)
  local copies, waits for them, and re-layouts  7.36 us (11%)
  between operations  1.29 us (2%)
    pallas_call x1, Pallas kernels, body(): pl.pallas_call(functools.partial(kernel, (lats, lons, row)), out_shape=(f...  57.7 us
    unnamed x11, local copies, waits for them, and re-layouts  6.6 us

profile of v1, /device:TPU:1, one launch (start us, length us, event | category | flops | bytes accessed | tf_op | source)
XLA Modules:
  0.0 66.4 jit_solution(705876270676074288)
XLA Ops:
  1.3 0.8 %copy.9.near_ref = s32[6,4]{1,0:T(8,128)S(1)} copy(s32[6,4]{0,1:T(4,128)} %bitcast.15) | data formatting | bytes 192 | tf_op jit(solution)/shard_map/squeeze | solution.py:348
  2.0 0.7 %copy.12 = f32[1,1,6,256]{3,2,1,0:T(8,128)S(1)} copy(f32[1,1,6,256]{3,1,2,0:T(1,128)} %param.8) | data formatting | bytes 12288
  2.7 0.0 copy-start
  2.7 1.9 %copy-done = bf16[1,1,6,4,256,256]{5,4,3,2,1,0:T(8,128)(2,1)S(1)} copy-done((bf16[1,1,6,4,256,256]{5,4,3,2,1,0:T(8,128)(2,1)S(1)}, bf16[1,1,6,4,256,256]{5,4,3,2,1,0:T(8,128)(2,1)}, u32[]{:S(2)}) %copy-start) | copy-done | bytes 3145752
  4.6 0.0 copy-start.1
  4.6 1.1 %copy-done.1 = bf16[1,1,6,256,256]{4,3,2,1,0:T(8,128)(2,1)S(1)} copy-done((bf16[1,1,6,256,256]{4,3,2,1,0:T(8,128)(2,1)S(1)}, bf16[1,1,6,256,256]{4,3,2,1,0:T(8,128)(2,1)}, u32[]{:S(2)}) %copy-start.1) | copy-done | bytes 786456
  5.8 0.0 copy-start.2
  5.8 0.9 %copy-done.2 = f32[1,1,6,16,256]{4,3,2,1,0:T(8,128)S(1)} copy-done((f32[1,1,6,16,256]{4,3,2,1,0:T(8,128)S(1)}, f32[1,1,6,16,256]{4,3,2,1,0:T(8,128)}, u32[]{:S(2)}) %copy-start.2) | copy-done | bytes 98328
  6.7 0.0 copy-start.3
  6.7 0.7 %copy-done.3 = s32[3072]{0:T(1024)S(1)} copy-done((s32[3072]{0:T(1024)S(1)}, s32[3072]{0:T(1024)}, u32[]{:S(2)}) %copy-start.3) | copy-done | bytes 12312
  7.4 57.7 %shard_map.86 = (f32[6,16,256]{2,1,0:T(8,128)S(1)}, f32[6,16,256]{2,1,0:T(8,128)S(1)}) custom-call(f32[6,16,256]{2,1,0:T(8,128)S(1)} %bitcast.13, f32[6,256]{1,0:T(8,128)S(1)} %bitcast.14, bf16[6,256,256]{2,1,0:T(8,128)(2,1)S(1)} %bitcast.10, bf16[6,4,256,256]{3,2,1,0:T(8,128)(2,1)S(1)} %bitcast.9, s32[6,4]{1,0:T(8,128)S(1)} %copy.9.near_ref, ...), custom_call_target="tpu_custom_call" | custom-call | tf_op jit(solution)/shard_map/pallas_call | solution.py:317
  65.1 0.6 copy.16
  65.7 0.6 copy.17
Async XLA Ops:
  2.7 1.9 %copy-start = (bf16[1,1,6,4,256,256]{5,4,3,2,1,0:T(8,128)(2,1)S(1)}, bf16[1,1,6,4,256,256]{5,4,3,2,1,0:T(8,128)(2,1)}, u32[]{:S(2)}) copy-start(bf16[1,1,6,4,256,256]{5,4,3,2,1,0:T(8,128)(2,1)} %param.10) | copy-start | bytes 9437188
  4.6 1.1 %copy-start.1 = (bf16[1,1,6,256,256]{4,3,2,1,0:T(8,128)(2,1)S(1)}, bf16[1,1,6,256,256]{4,3,2,1,0:T(8,128)(2,1)}, u32[]{:S(2)}) copy-start(bf16[1,1,6,256,256]{4,3,2,1,0:T(8,128)(2,1)} %param.9) | copy-start | bytes 2359300
  5.8 0.9 %copy-start.2 = (f32[1,1,6,16,256]{4,3,2,1,0:T(8,128)S(1)}, f32[1,1,6,16,256]{4,3,2,1,0:T(8,128)}, u32[]{:S(2)}) copy-start(f32[1,1,6,16,256]{4,3,2,1,0:T(8,128)} %param.7) | copy-start | bytes 294916
  6.7 0.7 %copy-start.3 = (s32[3072]{0:T(1024)S(1)}, s32[3072]{0:T(1024)}, u32[]{:S(2)}) copy-start(s32[3072]{0:T(1024)} %owner_ref.1) | copy-start | bytes 36868

commit v2 on v1

--- a/solution.py
+++ b/solution.py
@@ -9,8 +9,7 @@
 
 ROW = 16
 LANES = 128
-SMALL = 2.0**-75
-NEAR = (0, 1, 2, 3, 5, 6, 7, 8)
+NEAR = (3, 5, 0, 2, 6, 8, 1, 7)
 
 
 def dot(a, b):
@@ -23,9 +22,9 @@
 
 def kernel(
     sizes,
-    rhs_hbm, pre_hbm, fac_hbm, kri_hbm, near_ref, owner_ref, count_ref,
+    rhs_hbm, pre_hbm, fac_hbm, kri_hbm, near_hbm, owner_hbm, count_hbm,
     sol_ref, res_ref,
-    rhs, pre, fac, kri, lifted, halo, spread, select, out, arrive, row_sum, col_sum,
+    rhs, pre, fac, kri, near_ref, owner_ref, count_ref, whitened, halo, spread, select, out, arrive, row_sum, col_sum,
     load_sem, halo_send, halo_recv, back_send, back_recv, row_send, row_recv, col_send, col_recv,
 ):
     lats, lons, row = sizes
@@ -39,6 +38,9 @@
     block = lat * wide + place
 
     loads = [
+        pltpu.make_async_copy(near_hbm, near_ref, load_sem.at[4]),
+        pltpu.make_async_copy(owner_hbm, owner_ref, load_sem.at[5]),
+        pltpu.make_async_copy(count_hbm, count_ref, load_sem.at[6]),
         pltpu.make_async_copy(rhs_hbm, rhs, load_sem.at[0]),
         pltpu.make_async_copy(pre_hbm, pre, load_sem.at[1]),
         pltpu.make_async_copy(kri_hbm, kri, load_sem.at[2]),
@@ -49,9 +51,7 @@
 
     def beside(r):
         up, side = r // 3 - 1, r % 3 - 1
-        there = lat + up
-        valid = jnp.logical_and(there >= 0, there < lats)
-        return valid, (there, lax.rem(lon + side + lons, lons))
+        return lax.rem(lat + up + lats, lats), lax.rem(lon + side + lons, lons)
 
     def row_mate(step):
         return (lat, place * row + lax.rem(ring + step, row))
@@ -68,20 +68,20 @@
     def greet(device):
         pl.semaphore_signal(barrier, inc=1, device_id=device, device_id_type=pl.DeviceIdType.MESH)
 
+    for r in NEAR:
+        greet(beside(r))
     for step in far_first(row):
         greet(row_mate(step))
     for step in far_first(cols):
         greet(col_mate(step))
-    for r in NEAR:
-        valid, device = beside(r)
-        pl.when(valid)(functools.partial(greet, device))
-    edge = jnp.logical_or(lat == 0, lat == lats - 1)
-    around = jnp.where(edge, 5, 8)
+
+    for load in loads[:3]:
+        load.wait()
 
     wanted = []
     for b in range(slots):
         for m in range(links):
-            position = owner_ref[near_ref[b, m]]
+            position = owner_ref[near_ref[m, b]]
             region = position // slots
             slot = position - region * slots
             region_lat = region // lons
@@ -101,18 +101,6 @@
         rows = lax.broadcasted_iota(jnp.int32, (high, depth), 0) + r * high
         select[r] = jnp.where(rows == goal, 1.0, 0.0).astype(jnp.bfloat16)
 
-    @pl.when(lat == 0)
-    def _():
-        for k in range(2):
-            arrive[k, 0:3] = jnp.zeros((3, high, width), jnp.bfloat16)
-            halo[k, 0 : 3 * slots] = jnp.zeros((3 * slots, samples, width), jnp.bfloat16)
-
-    @pl.when(lat == lats - 1)
-    def _():
-        for k in range(2):
-            arrive[k, 6:9] = jnp.zeros((3, high, width), jnp.bfloat16)
-            halo[k, 6 * slots : 9 * slots] = jnp.zeros((3 * slots, samples, width), jnp.bfloat16)
-
     def remote(source, target, send, recv, device):
         return pltpu.make_async_remote_copy(
             src_ref=source, dst_ref=target, send_sem=send, recv_sem=recv,
@@ -120,41 +108,33 @@
         )
 
     def halo_copy(k, r):
-        valid, device = beside(r)
-        copy = remote(
+        return remote(
             halo.at[k, pl.ds(4 * slots, slots)], halo.at[k, pl.ds((8 - r) * slots, slots)],
-            halo_send.at[k, r], halo_recv.at[k, 8 - r], device,
+            halo_send.at[k, r], halo_recv.at[k, 8 - r], beside(r),
         )
-        return valid, copy
 
     def halo_arrival(k, r):
-        valid, device = beside(r)
         here = halo.at[k, pl.ds(r * slots, slots)]
-        return valid, remote(here, here, halo_send.at[k, r], halo_recv.at[k, r], device)
+        return remote(here, here, halo_send.at[k, r], halo_recv.at[k, r], beside(r))
 
     def back_copy(k, r):
-        valid, device = beside(r)
-        copy = remote(
-            out.at[k, r], arrive.at[k, 8 - r], back_send.at[k, r], back_recv.at[k, 8 - r], device
+        return remote(
+            out.at[k, r], arrive.at[k, 8 - r], back_send.at[k, r], back_recv.at[k, 8 - r], beside(r)
         )
-        return valid, copy
 
     def back_arrival(k, r):
-        valid, device = beside(r)
         here = arrive.at[k, r]
-        return valid, remote(here, here, back_send.at[k, r], back_recv.at[k, r], device)
+        return remote(here, here, back_send.at[k, r], back_recv.at[k, r], beside(r))
 
     def send_field(k, parts):
         for b in range(slots):
             halo[k, 4 * slots + b] = parts[b].astype(jnp.bfloat16)
         for r in NEAR:
-            valid, copy = halo_copy(k, r)
-            pl.when(valid)(copy.start)
+            halo_copy(k, r).start()
 
     def gather(k):
         for r in NEAR:
-            valid, copy = halo_arrival(k, r)
-            pl.when(valid)(copy.wait_recv)
+            halo_arrival(k, r).wait_recv()
         parts = []
         for b in range(slots):
             total = jnp.zeros((samples, width), jnp.float32)
@@ -178,15 +158,13 @@
         terms = spread[...]
         for r in NEAR:
             out[k, r] = dot(select[r], terms).astype(jnp.bfloat16)
-            valid, copy = back_copy(k, r)
-            pl.when(valid)(copy.start)
+            back_copy(k, r).start()
         mine = dot(select[4], terms)
         return [backs[b] + mine[b * samples : (b + 1) * samples] for b in range(slots)]
 
     def take_back(k, parts):
         for r in NEAR:
-            valid, copy = back_arrival(k, r)
-            pl.when(valid)(copy.wait_recv)
+            back_arrival(k, r).wait_recv()
         total = list(parts)
         for r in NEAR:
             for b in range(slots):
@@ -242,65 +220,62 @@
         many = col_sum.at[k, pl.ds(0, cols - 1)]
         remote(many, many, col_send.at[k], col_recv.at[k], col_mate(1)).wait_send()
 
-    loads[0].wait()
-    loads[1].wait()
+    loads[3].wait()
+    loads[4].wait()
     each = range(slots)
     source = [rhs[b] * live[b] for b in each]
-    scale = [pre[b : b + 1] for b in each]
+    scale = [pre[b] for b in each]
     first = [scale[b] * source[b] for b in each]
-    pl.semaphore_wait(barrier, row - 1 + cols - 1 + around)
+    pl.semaphore_wait(barrier, row - 1 + cols - 1 + len(NEAR))
     send_field(0, first)
-    loads[2].wait()
-    loads[3].wait()
+    loads[5].wait()
+    loads[6].wait()
 
     away = gather(0)
+    white = whiten([first[b].astype(jnp.bfloat16).astype(jnp.float32) - away[b] for b in each])
     for b in each:
-        lifted[b] = first[b].astype(jnp.bfloat16).astype(jnp.float32) - away[b]
-    image = send_back(0, whiten([lifted[b] for b in each]))
+        whitened[b] = white[b]
+    image = send_back(0, white)
+    sum_first(0, [inner(source, first), inner(white, white) + inner(first, first)])
     image = take_back(0, image)
     image = [image[b] + first[b] for b in each]
 
     scaled = [scale[b] * image[b] for b in each]
-    less = [SMALL * image[b] for b in each]
-    columns = [
-        inner(source, first),
-        inner(first, image),
-        inner(image, scaled),
-        inner(less, [SMALL * scaled[b] for b in each]),
-    ]
-    sum_first(0, columns)
     send_field(1, scaled)
+    slope_seen = inner(first, image)
     sum_second(0)
     away = gather(1)
-    current, slope, bend, bend_less = sum_last(0, 4)
+    current, slope = sum_last(0, 2)
     alpha = current / slope
-    more = alpha * (1.0 / SMALL)
-    square = jnp.where(bend < 3e38, (alpha * bend) * alpha, (more * bend_less) * more)
-    following = current - 2.0 * alpha * slope + square
-    beta = following / current
-    second = [(first[b] - alpha * scaled[b]) + beta * first[b] for b in each]
     parts = [
-        (1.0 + beta) * lifted[b] - alpha * (scaled[b].astype(jnp.bfloat16).astype(jnp.float32) - away[b])
-        for b in each
+        alpha * (scaled[b].astype(jnp.bfloat16).astype(jnp.float32) - away[b]) for b in each
     ]
     white = whiten(parts)
-    sum_first(1, [inner(white, white) + inner(second, second)])
+    scaled = [alpha * scaled[b] for b in each]
+    columns = [
+        slope_seen,
+        inner([alpha * image[b] for b in each], scaled),
+        inner([whitened[b] for b in each], white) + inner(first, scaled),
+        inner(white, white) + inner(scaled, scaled),
+    ]
+    sum_first(1, columns)
     turned = send_back(1, white)
-    residual = [source[b] - alpha * image[b] for b in each]
     sum_second(1)
     turned = take_back(1, turned)
-    [slope] = sum_last(1, 1)
-    step_size = following / slope
+    turned = [turned[b] + scaled[b] for b in each]
+    slope_seen, bend, mixed, last = sum_last(1, 4)
+    following = current - 2.0 * (alpha * slope_seen) + bend
+    grown = 1.0 + following / current
+    step_size = following / (grown * (grown * slope - 2.0 * mixed) + last)
+    along = alpha + step_size * grown
     for b in each:
-        sol_ref[b] = alpha * first[b] + step_size * second[b]
-        res_ref[b] = residual[b] - step_size * (turned[b] + second[b])
+        sol_ref[b] = along * first[b] - step_size * scaled[b]
+        res_ref[b] = source[b] - along * image[b] + step_size * turned[b]
 
     for k in range(2):
         for r in NEAR:
-            valid, copy = halo_copy(k, r)
-            pl.when(valid)(copy.wait_send)
-            valid, copy = back_copy(k, r)
-            pl.when(valid)(copy.wait_send)
+            halo_copy(k, r).wait_send()
+            back_copy(k, r).wait_send()
         sums_sent(k)
 
 
@@ -311,19 +286,21 @@
     cols = lats * (lons // row)
     high = slots * samples
     field = jax.ShapeDtypeStruct((slots, samples, width), jnp.float32)
-    anywhere = pl.BlockSpec(memory_space=pl.ANY)
-    scalars = pl.BlockSpec(memory_space=pltpu.SMEM)
+    far = pl.BlockSpec(memory_space=pl.ANY)
     vmem = pl.BlockSpec(memory_space=pltpu.VMEM)
     solved, left = pl.pallas_call(
         functools.partial(kernel, (lats, lons, row)),
         out_shape=(field, field),
-        in_specs=[anywhere] * 4 + [scalars] * 3,
+        in_specs=[far] * 7,
         out_specs=(vmem, vmem),
         scratch_shapes=[
             pltpu.VMEM((slots, samples, width), jnp.float32),
-            pltpu.VMEM((slots, width), jnp.float32),
+            pltpu.VMEM((slots, 1, width), jnp.float32),
             pltpu.VMEM((slots, width, width), jnp.bfloat16),
             pltpu.VMEM((slots, links, width, width), jnp.bfloat16),
+            pltpu.SMEM((links, slots), jnp.int32),
+            pltpu.SMEM(owner.shape, jnp.int32),
+            pltpu.SMEM((1, 1), jnp.int32),
             pltpu.VMEM((slots, samples, width), jnp.float32),
             pltpu.VMEM((2, 9 * slots, samples, width), jnp.bfloat16),
             pltpu.VMEM((slots * links * samples, width), jnp.bfloat16),
@@ -332,7 +309,7 @@
             pltpu.VMEM((2, 9, high, width), jnp.bfloat16),
             pltpu.VMEM((2, row, 1, LANES), jnp.float32),
             pltpu.VMEM((2, cols, 1, LANES), jnp.float32),
-            pltpu.SemaphoreType.DMA((4,)),
+            pltpu.SemaphoreType.DMA((7,)),
             pltpu.SemaphoreType.DMA((2, 9)),
             pltpu.SemaphoreType.DMA((2, 9)),
             pltpu.SemaphoreType.DMA((2, 9)),
@@ -345,7 +322,16 @@
         compiler_params=pltpu.CompilerParams(
             collective_id=0, has_side_effects=True, vmem_limit_bytes=32 * 2**20
         ),
-    )(rhs[0, 0], precond[0, 0], factor[0, 0], kriging[0, 0], neighbours[0, 0], owner, counts)
+    )(
+        *(
+            pltpu.with_memory_space_constraint(a, pltpu.HBM)
+            for a in (
+                rhs[0, 0], precond.reshape(slots, 1, width), factor[0, 0], kriging[0, 0],
+                neighbours[0, 0].T, owner,
+            )
+        ),
+        counts,
+    )
     return solved[None, None], left[None, None]
 
 

time: 66.7 us -> 55 us (0.82)
  local copies, waits for them, and re-layouts: 7.36 us -> 1.28 us
  Pallas kernels: 57.7 us -> 52.3 us
    pallas_call x1, Pallas kernels: 57.7 us -> 52.3 us  [body(): pl.pallas_call(functools.partial(kernel, (lats, lons, row)), out_shape=(f...]
    unnamed x11 -> x2, local copies, waits for them, and re-layouts: 6.6 us -> 1.28 us
    squeeze x1 -> x0, local copies, waits for them, and re-layouts: 0.77 us -> none  [body(): neighbours[0, 0]]
where the time goes in v2:
time: 55 us; the launch traced here: 54.8 us
  Pallas kernels  52.3 us (95%)
  between operations  1.29 us (2%)
  local copies, waits for them, and re-layouts  1.28 us (2%)
    pallas_call x1, Pallas kernels, body(): pl.pallas_call(functools.partial(kernel, (lats, lons, row)), out_shape=(f...  52.3 us
    unnamed x2, local copies, waits for them, and re-layouts  1.28 us

profile of v2, /device:TPU:1, one launch (start us, length us, event | category | flops | bytes accessed | tf_op | source)
XLA Modules:
  0.0 54.8 jit_solution(739023392078848543)
XLA Ops:
  1.3 52.3 %shard_map.86 = (f32[6,16,256]{2,1,0:T(8,128)S(1)}, f32[6,16,256]{2,1,0:T(8,128)S(1)}) custom-call(f32[6,16,256]{2,1,0:T(8,128)} %bitcast.13, f32[6,1,256]{2,1,0:T(1,128)} %bitcast.14, bf16[6,256,256]{2,1,0:T(8,128)(2,1)} %bitcast.12, bf16[6,4,256,256]{3,2,1,0:T(8,128)(2,1)} %bitcast.11, s32[4,6]{1,0:T(4,128)} %bitcast.15, s32[3072]{0:T(1024)} %owner_hbm.1, ...), custom_call_target="tpu_custom_call" | custom-call | tf_op jit(solution)/shard_map/pallas_call | solution.py:291
  53.6 0.6 %copy.12 = f32[1,1,6,16,256]{4,3,2,1,0:T(8,128)} copy(f32[1,1,6,16,256]{4,3,2,1,0:T(8,128)S(1)} %bitcast.10) | data formatting | bytes 196608
  54.2 0.6 %copy.13 = f32[1,1,6,16,256]{4,3,2,1,0:T(8,128)} copy(f32[1,1,6,16,256]{4,3,2,1,0:T(8,128)S(1)} %bitcast.9) | data formatting | bytes 196608

commit v3 on v2

--- a/solution.py
+++ b/solution.py
@@ -9,7 +9,7 @@
 
 ROW = 16
 LANES = 128
-NEAR = (3, 5, 0, 2, 6, 8, 1, 7)
+REACH = 4
 
 
 def dot(a, b):
@@ -24,8 +24,10 @@
     sizes,
     rhs_hbm, pre_hbm, fac_hbm, kri_hbm, near_hbm, owner_hbm, count_hbm,
     sol_ref, res_ref,
-    rhs, pre, fac, kri, near_ref, owner_ref, count_ref, whitened, halo, spread, select, out, arrive, row_sum, col_sum,
-    load_sem, halo_send, halo_recv, back_send, back_recv, row_send, row_recv, col_send, col_recv,
+    rhs, pre, fac, kri, near_ref, owner_ref, count_ref, turned_kri, whitened, halo, spread, select,
+    out, arrive, relay, row_sum, col_sum,
+    load_sem, halo_send, halo_recv, back_send, back_recv,
+    relay_send, relay_recv, far_sem, row_send, row_recv, col_send, col_recv,
 ):
     lats, lons, row = sizes
     slots, samples, width = rhs.shape
@@ -49,9 +51,14 @@
     for load in loads:
         load.start()
 
-    def beside(r):
-        up, side = r // 3 - 1, r % 3 - 1
+    def beside(up, side):
         return lax.rem(lat + up + lats, lats), lax.rem(lon + side + lons, lons)
+
+    def at(up, side):
+        return (up + 1) * 3 + side + 1
+
+    mate = 1 - 2 * lax.rem(lat, 2)
+    near = [(0, -1), (0, 1), (-mate, -1), (-mate, 1), (mate, 0), (-mate, 0)]
 
     def row_mate(step):
         return (lat, place * row + lax.rem(ring + step, row))
@@ -68,9 +75,10 @@
     def greet(device):
         pl.semaphore_signal(barrier, inc=1, device_id=device, device_id_type=pl.DeviceIdType.MESH)
 
-    for r in NEAR:
-        greet(beside(r))
-    for step in far_first(row):
+    close = [step for step in far_first(row) if min(step, row - step) <= REACH]
+    for up, side in near:
+        greet(beside(up, side))
+    for step in close:
         greet(row_mate(step))
     for step in far_first(cols):
         greet(col_mate(step))
@@ -107,39 +115,57 @@
             device_id=device, device_id_type=pl.DeviceIdType.MESH,
         )
 
-    def halo_copy(k, r):
+    def halo_copy(k, up, side):
+        own = halo.at[k, pl.ds(4 * slots, slots)]
+        there = halo.at[k, pl.ds(at(-up, -side) * slots, slots)]
+        send, recv = halo_send.at[k, at(up, side)], halo_recv.at[k, at(-up, -side)]
+        return remote(own, there, send, recv, beside(up, side))
+
+    def halo_relay(k, side):
+        own = halo.at[k, pl.ds(at(0, side) * slots, slots)]
+        there = halo.at[k, pl.ds(at(-mate, side) * slots, slots)]
+        send, recv = halo_send.at[k, at(mate, side)], halo_recv.at[k, at(-mate, side)]
+        return remote(own, there, send, recv, beside(mate, 0))
+
+    def halo_arrival(k, up, side):
+        here = halo.at[k, pl.ds(at(up, side) * slots, slots)]
+        send, recv = halo_send.at[k, at(up, side)], halo_recv.at[k, at(up, side)]
+        return remote(here, here, send, recv, beside(0, 1))
+
+    def back_copy(k, up, side):
+        send, recv = back_send.at[k, at(up, side)], back_recv.at[k, at(-up, -side)]
+        own, there = out.at[k, at(up, side)], arrive.at[k, at(-up, -side)]
+        return remote(own, there, send, recv, beside(up, side))
+
+    def back_arrival(k, up, side):
+        here = arrive.at[k, at(up, side)]
+        send, recv = back_send.at[k, at(up, side)], back_recv.at[k, at(up, side)]
+        return remote(here, here, send, recv, beside(0, 1))
+
+    def back_relay(k, side):
+        i = (side + 1) // 2
         return remote(
-            halo.at[k, pl.ds(4 * slots, slots)], halo.at[k, pl.ds((8 - r) * slots, slots)],
-            halo_send.at[k, r], halo_recv.at[k, 8 - r], beside(r),
+            out.at[k, at(mate, side)], relay.at[k, i], relay_send.at[k, i], relay_recv.at[k, i],
+            beside(mate, 0),
         )
-
-    def halo_arrival(k, r):
-        here = halo.at[k, pl.ds(r * slots, slots)]
-        return remote(here, here, halo_send.at[k, r], halo_recv.at[k, r], beside(r))
-
-    def back_copy(k, r):
-        return remote(
-            out.at[k, r], arrive.at[k, 8 - r], back_send.at[k, r], back_recv.at[k, 8 - r], beside(r)
-        )
-
-    def back_arrival(k, r):
-        here = arrive.at[k, r]
-        return remote(here, here, back_send.at[k, r], back_recv.at[k, r], beside(r))
 
     def send_field(k, parts):
         for b in range(slots):
             halo[k, 4 * slots + b] = parts[b].astype(jnp.bfloat16)
-        for r in NEAR:
-            halo_copy(k, r).start()
+        for up, side in near:
+            halo_copy(k, up, side).start()
 
     def gather(k):
-        for r in NEAR:
-            halo_arrival(k, r).wait_recv()
+        for side in (-1, 1):
+            halo_arrival(k, 0, side).wait_recv()
+            halo_relay(k, side).start()
+        for up, side in near[2:] + [(mate, -1), (mate, 1)]:
+            halo_arrival(k, up, side).wait_recv()
         parts = []
         for b in range(slots):
             total = jnp.zeros((samples, width), jnp.float32)
             for m in range(links):
-                total = total + dot_t(halo[k, wanted[b * links + m]], kri[b, m])
+                total = total + dot(halo[k, wanted[b * links + m]], turned_kri[b, m])
             parts.append(total)
         return parts
 
@@ -156,19 +182,28 @@
                 i = b * links + m
                 spread[i * samples : (i + 1) * samples] = (-dot(low, kri[b, m])).astype(jnp.bfloat16)
         terms = spread[...]
-        for r in NEAR:
-            out[k, r] = dot(select[r], terms).astype(jnp.bfloat16)
-            back_copy(k, r).start()
+        for side in (-1, 1):
+            out[k, at(mate, side)] = dot(select[at(mate, side)], terms).astype(jnp.bfloat16)
+            back_relay(k, side).start()
+        for up, side in near[2:]:
+            out[k, at(up, side)] = dot(select[at(up, side)], terms).astype(jnp.bfloat16)
+            back_copy(k, up, side).start()
+        for side in (-1, 1):
+            straight = dot(select[at(0, side)], terms)
+            back_relay(k, side).wait_recv()
+            both = straight + relay[k, (side + 1) // 2].astype(jnp.float32)
+            out[k, at(0, side)] = both.astype(jnp.bfloat16)
+            back_copy(k, 0, side).start()
         mine = dot(select[4], terms)
         return [backs[b] + mine[b * samples : (b + 1) * samples] for b in range(slots)]
 
     def take_back(k, parts):
-        for r in NEAR:
-            back_arrival(k, r).wait_recv()
+        for up, side in near:
+            back_arrival(k, up, side).wait_recv()
         total = list(parts)
-        for r in NEAR:
+        for up, side in near:
             for b in range(slots):
-                piece = arrive[k, r, b * samples : (b + 1) * samples]
+                piece = arrive[k, at(up, side), b * samples : (b + 1) * samples]
                 total[b] = total[b] + piece.astype(jnp.float32)
         return total
 
@@ -226,16 +261,26 @@
     source = [rhs[b] * live[b] for b in each]
     scale = [pre[b] for b in each]
     first = [scale[b] * source[b] for b in each]
-    pl.semaphore_wait(barrier, row - 1 + cols - 1 + len(NEAR))
+    pl.semaphore_wait(barrier, len(near) + len(close) + cols - 1)
     send_field(0, first)
+    if len(close) < row - 1:
+        for step in (REACH, row - REACH):
+            pl.semaphore_signal(
+                far_sem, inc=1, device_id=row_mate(step), device_id_type=pl.DeviceIdType.MESH
+            )
     loads[5].wait()
     loads[6].wait()
+    for b in each:
+        for m in range(links):
+            turned_kri[b, m] = kri[b, m].T
 
     away = gather(0)
     white = whiten([first[b].astype(jnp.bfloat16).astype(jnp.float32) - away[b] for b in each])
     for b in each:
         whitened[b] = white[b]
     image = send_back(0, white)
+    if len(close) < row - 1:
+        pl.semaphore_wait(far_sem, 2)
     sum_first(0, [inner(source, first), inner(white, white) + inner(first, first)])
     image = take_back(0, image)
     image = [image[b] + first[b] for b in each]
@@ -273,9 +318,12 @@
         res_ref[b] = source[b] - along * image[b] + step_size * turned[b]
 
     for k in range(2):
-        for r in NEAR:
-            halo_copy(k, r).wait_send()
-            back_copy(k, r).wait_send()
+        for up, side in near:
+            halo_copy(k, up, side).wait_send()
+            back_copy(k, up, side).wait_send()
+        for side in (-1, 1):
+            halo_relay(k, side).wait_send()
+            back_relay(k, side).wait_send()
         sums_sent(k)
 
 
@@ -301,12 +349,14 @@
             pltpu.SMEM((links, slots), jnp.int32),
             pltpu.SMEM(owner.shape, jnp.int32),
             pltpu.SMEM((1, 1), jnp.int32),
+            pltpu.VMEM((slots, links, width, width), jnp.bfloat16),
             pltpu.VMEM((slots, samples, width), jnp.float32),
             pltpu.VMEM((2, 9 * slots, samples, width), jnp.bfloat16),
             pltpu.VMEM((slots * links * samples, width), jnp.bfloat16),
             pltpu.VMEM((9, high, slots * links * samples), jnp.bfloat16),
             pltpu.VMEM((2, 9, high, width), jnp.bfloat16),
             pltpu.VMEM((2, 9, high, width), jnp.bfloat16),
+            pltpu.VMEM((2, 2, high, width), jnp.bfloat16),
             pltpu.VMEM((2, row, 1, LANES), jnp.float32),
             pltpu.VMEM((2, cols, 1, LANES), jnp.float32),
             pltpu.SemaphoreType.DMA((7,)),
@@ -314,6 +364,9 @@
             pltpu.SemaphoreType.DMA((2, 9)),
             pltpu.SemaphoreType.DMA((2, 9)),
             pltpu.SemaphoreType.DMA((2, 9)),
+            pltpu.SemaphoreType.DMA((2, 2)),
+            pltpu.SemaphoreType.DMA((2, 2)),
+            pltpu.SemaphoreType.REGULAR,
             pltpu.SemaphoreType.DMA((2,)),
             pltpu.SemaphoreType.DMA((2,)),
             pltpu.SemaphoreType.DMA((2,)),

time: 55 us -> 52.5 us (0.955)
  Pallas kernels: 52.3 us -> 49.8 us
    pallas_call x1, Pallas kernels: 52.3 us -> 49.8 us  [body(): pl.pallas_call(functools.partial(kernel, (lats, lons, row)), out_shape=(f...]
where the time goes in v3:
time: 52.5 us; the launch traced here: 52.3 us
  Pallas kernels  49.8 us (95%)
  between operations  1.29 us (2%)
  local copies, waits for them, and re-layouts  1.28 us (2%)
    pallas_call x1, Pallas kernels, body(): pl.pallas_call(functools.partial(kernel, (lats, lons, row)), out_shape=(f...  49.8 us
    unnamed x2, local copies, waits for them, and re-layouts  1.28 us

profile of v3, /device:TPU:1, one launch (start us, length us, event | category | flops | bytes accessed | tf_op | source)
XLA Modules:
  0.0 52.3 jit_solution(12406521192380283685)
XLA Ops:
  1.3 49.8 %shard_map.86 = (f32[6,16,256]{2,1,0:T(8,128)S(1)}, f32[6,16,256]{2,1,0:T(8,128)S(1)}) custom-call(f32[6,16,256]{2,1,0:T(8,128)} %bitcast.13, f32[6,1,256]{2,1,0:T(1,128)} %bitcast.14, bf16[6,256,256]{2,1,0:T(8,128)(2,1)} %bitcast.12, bf16[6,4,256,256]{3,2,1,0:T(8,128)(2,1)} %bitcast.11, s32[4,6]{1,0:T(4,128)} %bitcast.15, s32[3072]{0:T(1024)} %owner_hbm.1, ...), custom_call_target="tpu_custom_call" | custom-call | tf_op jit(solution)/shard_map/pallas_call | solution.py:339
  51.0 0.6 %copy.12 = f32[1,1,6,16,256]{4,3,2,1,0:T(8,128)} copy(f32[1,1,6,16,256]{4,3,2,1,0:T(8,128)S(1)} %bitcast.10) | data formatting | bytes 196608
  51.7 0.6 %copy.13 = f32[1,1,6,16,256]{4,3,2,1,0:T(8,128)} copy(f32[1,1,6,16,256]{4,3,2,1,0:T(8,128)S(1)} %bitcast.9) | data formatting | bytes 196608

commit v4 on v3

--- a/solution.py
+++ b/solution.py
@@ -9,7 +9,7 @@
 
 ROW = 16
 LANES = 128
-REACH = 4
+REACH = 2
 
 
 def dot(a, b):
@@ -23,11 +23,11 @@
 def kernel(
     sizes,
     rhs_hbm, pre_hbm, fac_hbm, kri_hbm, near_hbm, owner_hbm, count_hbm,
-    sol_ref, res_ref,
+    first_ref, scaled_ref, source_ref, image_ref, turned_ref, along_ref, step_ref,
     rhs, pre, fac, kri, near_ref, owner_ref, count_ref, turned_kri, whitened, halo, spread, select,
     out, arrive, relay, row_sum, col_sum,
     load_sem, halo_send, halo_recv, back_send, back_recv,
-    relay_send, relay_recv, far_sem, row_send, row_recv, col_send, col_recv,
+    relay_send, relay_recv, far_col, far_row, row_send, row_recv, col_send, col_recv,
 ):
     lats, lons, row = sizes
     slots, samples, width = rhs.shape
@@ -75,13 +75,29 @@
     def greet(device):
         pl.semaphore_signal(barrier, inc=1, device_id=device, device_id_type=pl.DeviceIdType.MESH)
 
-    close = [step for step in far_first(row) if min(step, row - step) <= REACH]
+    handed = lats == 8 and wide == 4 and row == 16
+    close = [step for step in far_first(row) if not handed or min(step, row - step) <= REACH]
+    mates = [
+        (core, x, y)
+        for x in range(lats // 2)
+        for y in range(wide)
+        for core in range(2)
+        if core + x + y > 0
+        and (not handed or min(x, lats // 2 - x) + min(y, wide - y) <= REACH)
+    ]
+
+    def block_mate(core, x, y):
+        other = lax.rem(lat % 2 + core, 2) + 2 * lax.rem(lat // 2 + x, lats // 2)
+        return other, lax.rem(place + y, wide) * row + ring
+
+    def tell(sem, device):
+        pl.semaphore_signal(sem, inc=1, device_id=device, device_id_type=pl.DeviceIdType.MESH)
     for up, side in near:
         greet(beside(up, side))
     for step in close:
         greet(row_mate(step))
-    for step in far_first(cols):
-        greet(col_mate(step))
+    for mate_of in mates:
+        greet(block_mate(*mate_of))
 
     for load in loads[:3]:
         load.wait()
@@ -172,7 +188,7 @@
     def whiten(parts):
         return [dot_t(parts[b].astype(jnp.bfloat16), fac[b]) * live[b] for b in range(slots)]
 
-    def send_back(k, white):
+    def send_back(k, white, between=lambda: None):
         backs = []
         for b in range(slots):
             back = dot(white[b].astype(jnp.bfloat16), fac[b])
@@ -181,6 +197,7 @@
             for m in range(links):
                 i = b * links + m
                 spread[i * samples : (i + 1) * samples] = (-dot(low, kri[b, m])).astype(jnp.bfloat16)
+        between()
         terms = spread[...]
         for side in (-1, 1):
             out[k, at(mate, side)] = dot(select[at(mate, side)], terms).astype(jnp.bfloat16)
@@ -229,21 +246,21 @@
         packed = jnp.zeros((samples, LANES), jnp.float32)
         for i, column in enumerate(columns):
             packed = packed + jnp.where(diagonal == i * samples, column, 0.0)
-        row_sum[k, ring] = jnp.sum(packed, axis=0, keepdims=True)
+        col_sum[k, block] = jnp.sum(packed, axis=0, keepdims=True)
+        for step in far_first(cols):
+            col_copy(k, step).start()
+
+    def sum_second(k):
+        many = col_sum.at[k, pl.ds(0, cols - 1)]
+        remote(many, many, col_send.at[k], col_recv.at[k], col_mate(1)).wait_recv()
+        row_sum[k, ring] = jnp.sum(col_sum[k], axis=0)
         for step in far_first(row):
             row_copy(k, step).start()
 
-    def sum_second(k):
+    def sum_last(k, n):
         many = row_sum.at[k, pl.ds(0, row - 1)]
         remote(many, many, row_send.at[k], row_recv.at[k], row_mate(1)).wait_recv()
-        col_sum[k, block] = jnp.sum(row_sum[k], axis=0)
-        for step in far_first(cols):
-            col_copy(k, step).start()
-
-    def sum_last(k, n):
-        many = col_sum.at[k, pl.ds(0, cols - 1)]
-        remote(many, many, col_send.at[k], col_recv.at[k], col_mate(1)).wait_recv()
-        total = jnp.broadcast_to(jnp.sum(col_sum[k], axis=0), (samples, LANES))
+        total = jnp.broadcast_to(jnp.sum(row_sum[k], axis=0), (samples, LANES))
         return [
             jnp.sum(jnp.where(diagonal == i * samples, total, 0.0), axis=1, keepdims=True)
             for i in range(n)
@@ -261,13 +278,13 @@
     source = [rhs[b] * live[b] for b in each]
     scale = [pre[b] for b in each]
     first = [scale[b] * source[b] for b in each]
-    pl.semaphore_wait(barrier, len(near) + len(close) + cols - 1)
+    pl.semaphore_wait(barrier, len(near) + len(close) + len(mates))
     send_field(0, first)
-    if len(close) < row - 1:
-        for step in (REACH, row - REACH):
-            pl.semaphore_signal(
-                far_sem, inc=1, device_id=row_mate(step), device_id_type=pl.DeviceIdType.MESH
-            )
+    if handed:
+        tell(far_col.at[0], block_mate(0, lats // 4, 0))
+        tell(far_col.at[0], block_mate(0, 0, wide // 2))
+        tell(far_row.at[0], row_mate(REACH))
+        tell(far_row.at[0], row_mate(row - REACH))
     loads[5].wait()
     loads[6].wait()
     for b in each:
@@ -275,20 +292,30 @@
             turned_kri[b, m] = kri[b, m].T
 
     away = gather(0)
+    if handed:
+        pl.semaphore_wait(far_row.at[0], 2)
+        tell(far_row.at[1], row_mate(2 * REACH))
+        tell(far_row.at[1], row_mate(row - 2 * REACH))
     white = whiten([first[b].astype(jnp.bfloat16).astype(jnp.float32) - away[b] for b in each])
     for b in each:
         whitened[b] = white[b]
-    image = send_back(0, white)
-    if len(close) < row - 1:
-        pl.semaphore_wait(far_sem, 2)
-    sum_first(0, [inner(source, first), inner(white, white) + inner(first, first)])
+    columns = [inner(source, first), inner(white, white) + inner(first, first)]
+
+    def early_sum():
+        if handed:
+            pl.semaphore_wait(far_col.at[0], 2)
+        sum_first(0, columns)
+
+    image = send_back(0, white, early_sum)
+    if handed:
+        pl.semaphore_wait(far_row.at[1], 2)
+    sum_second(0)
     image = take_back(0, image)
     image = [image[b] + first[b] for b in each]
 
     scaled = [scale[b] * image[b] for b in each]
     send_field(1, scaled)
     slope_seen = inner(first, image)
-    sum_second(0)
     away = gather(1)
     current, slope = sum_last(0, 2)
     alpha = current / slope
@@ -307,15 +334,18 @@
     turned = send_back(1, white)
     sum_second(1)
     turned = take_back(1, turned)
-    turned = [turned[b] + scaled[b] for b in each]
+    for b in each:
+        first_ref[b] = first[b]
+        scaled_ref[b] = scaled[b]
+        source_ref[b] = source[b]
+        image_ref[b] = image[b]
+        turned_ref[b] = turned[b] + scaled[b]
     slope_seen, bend, mixed, last = sum_last(1, 4)
     following = current - 2.0 * (alpha * slope_seen) + bend
     grown = 1.0 + following / current
     step_size = following / (grown * (grown * slope - 2.0 * mixed) + last)
-    along = alpha + step_size * grown
-    for b in each:
-        sol_ref[b] = along * first[b] - step_size * scaled[b]
-        res_ref[b] = source[b] - along * image[b] + step_size * turned[b]
+    along_ref[...] = jnp.broadcast_to(alpha + step_size * grown, (samples, width))
+    step_ref[...] = jnp.broadcast_to(step_size, (samples, width))
 
     for k in range(2):
         for up, side in near:
@@ -336,11 +366,11 @@
     field = jax.ShapeDtypeStruct((slots, samples, width), jnp.float32)
     far = pl.BlockSpec(memory_space=pl.ANY)
     vmem = pl.BlockSpec(memory_space=pltpu.VMEM)
-    solved, left = pl.pallas_call(
+    first, scaled, source, image, turned, along, step_size = pl.pallas_call(
         functools.partial(kernel, (lats, lons, row)),
-        out_shape=(field, field),
+        out_shape=(field,) * 5 + (jax.ShapeDtypeStruct((samples, width), jnp.float32),) * 2,
         in_specs=[far] * 7,
-        out_specs=(vmem, vmem),
+        out_specs=(vmem,) * 7,
         scratch_shapes=[
             pltpu.VMEM((slots, samples, width), jnp.float32),
             pltpu.VMEM((slots, 1, width), jnp.float32),
@@ -366,7 +396,8 @@
             pltpu.SemaphoreType.DMA((2, 9)),
             pltpu.SemaphoreType.DMA((2, 2)),
             pltpu.SemaphoreType.DMA((2, 2)),
-            pltpu.SemaphoreType.REGULAR,
+            pltpu.SemaphoreType.REGULAR((1,)),
+            pltpu.SemaphoreType.REGULAR((2,)),
             pltpu.SemaphoreType.DMA((2,)),
             pltpu.SemaphoreType.DMA((2,)),
             pltpu.SemaphoreType.DMA((2,)),
@@ -385,6 +416,8 @@
         ),
         counts,
     )
+    solved = along * first - step_size * scaled
+    left = source - along * image + step_size * turned
     return solved[None, None], left[None, None]
 
 

time: 52.5 us -> 48.9 us (0.931)
  Pallas kernels: 49.8 us -> 46.8 us
  local copies, waits for them, and re-layouts: 1.28 us -> 0 us
  other arithmetic: 0 us -> 0.71 us
    pallas_call x1, Pallas kernels: 49.8 us -> 46.8 us  [body(): pl.pallas_call(functools.partial(kernel, (lats, lons, row)), out_shape=(f...]
    unnamed x2 -> x0, local copies, waits for them, and re-layouts: 1.28 us -> none
    broadcast_in_dim x0 -> x1, other arithmetic: none -> 0.71 us  [body(): return (solved[None, None], left[None, None])]
where the time goes in v4:
time: 48.9 us; the launch traced here: 48.8 us
  Pallas kernels  46.8 us (96%)
  between operations  1.29 us (3%)
  other arithmetic  0.71 us (1%)
    pallas_call x1, Pallas kernels, body(): pl.pallas_call(functools.partial(kernel, (lats, lons, row)), out_shape=(f...  46.8 us

profile of v4, /device:TPU:1, one launch (start us, length us, event | category | flops | bytes accessed | tf_op | source)
XLA Modules:
  0.0 48.8 jit_solution(5846220899553580048)
XLA Ops:
  1.3 46.8 %shard_map.86 = (f32[6,16,256]{2,1,0:T(8,128)S(1)}, f32[6,16,256]{2,1,0:T(8,128)S(1)}, f32[6,16,256]{2,1,0:T(8,128)S(1)}, f32[6,16,256]{2,1,0:T(8,128)S(1)}, f32...) custom-call(f32[6,16,256]{2,1,0:T(8,128)} %bitcast.13, f32[6,1,256]{2,1,0:T(1,128)} %bitcast.14, ...), custom_call_target="tpu_custom_call" | custom-call | tf_op jit(solution)/shard_map/pallas_call | solution.py:369
  48.1 0.7 %add_bitcast_fusion = (f32[1,1,6,16,256]{4,3,2,1,0:T(8,128)}, f32[1,1,6,16,256]{4,3,2,1,0:T(8,128)}) fusion(f32[6,16,256]{2,1,0:T(8,128)S(1)} %get-tuple-element.15, f32[6,16,256]{2,1,0:T(8,128)S(1)} %get-tuple-element.13, f32[6,16,256]{2,1,0:T(8,128)S(1)} %get-tuple-element.14, f32[16,256]{1,0:T(8,128)S(1)} %get-tuple-element.11, ...), kind=kLoop, calls=%fused_computation | loop fusion | flops 172032 | bytes 720896 | tf_op jit(solution)/shard_map/broadcast_in_dim | solution.py:421

commit v5 on v4

--- a/solution.py
+++ b/solution.py
@@ -16,15 +16,11 @@
     return lax.dot_general(a, b, (((1,), (0,)), ((), ())), preferred_element_type=jnp.float32)
 
 
-def dot_t(a, b):
-    return lax.dot_general(a, b, (((1,), (1,)), ((), ())), preferred_element_type=jnp.float32)
-
-
 def kernel(
     sizes,
     rhs_hbm, pre_hbm, fac_hbm, kri_hbm, near_hbm, owner_hbm, count_hbm,
     first_ref, scaled_ref, source_ref, image_ref, turned_ref, along_ref, step_ref,
-    rhs, pre, fac, kri, near_ref, owner_ref, count_ref, turned_kri, whitened, halo, spread, select,
+    rhs, pre, fac, kri, near_ref, owner_ref, count_ref, turned_kri, turned_fac, whitened, halo, spread, select,
     out, arrive, relay, row_sum, col_sum,
     load_sem, halo_send, halo_recv, back_send, back_recv,
     relay_send, relay_recv, far_col, far_row, row_send, row_recv, col_send, col_recv,
@@ -40,13 +36,13 @@
     block = lat * wide + place
 
     loads = [
-        pltpu.make_async_copy(near_hbm, near_ref, load_sem.at[4]),
-        pltpu.make_async_copy(owner_hbm, owner_ref, load_sem.at[5]),
-        pltpu.make_async_copy(count_hbm, count_ref, load_sem.at[6]),
-        pltpu.make_async_copy(rhs_hbm, rhs, load_sem.at[0]),
-        pltpu.make_async_copy(pre_hbm, pre, load_sem.at[1]),
-        pltpu.make_async_copy(kri_hbm, kri, load_sem.at[2]),
-        pltpu.make_async_copy(fac_hbm, fac, load_sem.at[3]),
+        pltpu.make_async_copy(count_hbm, count_ref, load_sem.at[0]),
+        pltpu.make_async_copy(rhs_hbm, rhs, load_sem.at[1]),
+        pltpu.make_async_copy(pre_hbm, pre, load_sem.at[2]),
+        pltpu.make_async_copy(near_hbm, near_ref, load_sem.at[3]),
+        pltpu.make_async_copy(owner_hbm, owner_ref, load_sem.at[4]),
+        pltpu.make_async_copy(kri_hbm, kri, load_sem.at[5]),
+        pltpu.make_async_copy(fac_hbm, fac, load_sem.at[6]),
     ]
     for load in loads:
         load.start()
@@ -98,32 +94,6 @@
         greet(row_mate(step))
     for mate_of in mates:
         greet(block_mate(*mate_of))
-
-    for load in loads[:3]:
-        load.wait()
-
-    wanted = []
-    for b in range(slots):
-        for m in range(links):
-            position = owner_ref[near_ref[m, b]]
-            region = position // slots
-            slot = position - region * slots
-            region_lat = region // lons
-            up = region_lat - lat
-            side = lax.rem(region - region_lat * lons - lon + 1 + lons, lons)
-            index = ((up + 1) * 3 + side) * slots + slot
-            wanted.append(jnp.clip(index, 0, 9 * slots - 1))
-    live = [jnp.where(b < count_ref[0, 0], 1.0, 0.0).astype(jnp.float32) for b in range(slots)]
-
-    depth = slots * links * samples
-    lane = lax.broadcasted_iota(jnp.int32, (1, depth), 1)
-    link, sample = lane // samples, lane % samples
-    goal = sample
-    for i, w in enumerate(wanted):
-        goal = goal + jnp.where(link == i, w * samples, 0)
-    for r in range(9):
-        rows = lax.broadcasted_iota(jnp.int32, (high, depth), 0) + r * high
-        select[r] = jnp.where(rows == goal, 1.0, 0.0).astype(jnp.bfloat16)
 
     def remote(source, target, send, recv, device):
         return pltpu.make_async_remote_copy(
@@ -186,7 +156,7 @@
         return parts
 
     def whiten(parts):
-        return [dot_t(parts[b].astype(jnp.bfloat16), fac[b]) * live[b] for b in range(slots)]
+        return [dot(parts[b].astype(jnp.bfloat16), turned_fac[b]) * live[b] for b in range(slots)]
 
     def send_back(k, white, between=lambda: None):
         backs = []
@@ -272,9 +242,10 @@
         many = col_sum.at[k, pl.ds(0, cols - 1)]
         remote(many, many, col_send.at[k], col_recv.at[k], col_mate(1)).wait_send()
 
-    loads[3].wait()
-    loads[4].wait()
+    for load in loads[:3]:
+        load.wait()
     each = range(slots)
+    live = [jnp.where(b < count_ref[0, 0], 1.0, 0.0).astype(jnp.float32) for b in range(slots)]
     source = [rhs[b] * live[b] for b in each]
     scale = [pre[b] for b in each]
     first = [scale[b] * source[b] for b in each]
@@ -285,11 +256,38 @@
         tell(far_col.at[0], block_mate(0, 0, wide // 2))
         tell(far_row.at[0], row_mate(REACH))
         tell(far_row.at[0], row_mate(row - REACH))
+
+    loads[3].wait()
+    loads[4].wait()
+
+    wanted = []
+    for b in range(slots):
+        for m in range(links):
+            position = owner_ref[near_ref[m, b]]
+            region = position // slots
+            slot = position - region * slots
+            region_lat = region // lons
+            up = region_lat - lat
+            side = lax.rem(region - region_lat * lons - lon + 1 + lons, lons)
+            index = ((up + 1) * 3 + side) * slots + slot
+            wanted.append(jnp.clip(index, 0, 9 * slots - 1))
+    depth = slots * links * samples
+    lane = lax.broadcasted_iota(jnp.int32, (1, depth), 1)
+    link, sample = lane // samples, lane % samples
+    goal = sample
+    for i, w in enumerate(wanted):
+        goal = goal + jnp.where(link == i, w * samples, 0)
+    for r in range(9):
+        rows = lax.broadcasted_iota(jnp.int32, (high, depth), 0) + r * high
+        select[r] = jnp.where(rows == goal, 1.0, 0.0).astype(jnp.bfloat16)
+
     loads[5].wait()
-    loads[6].wait()
     for b in each:
         for m in range(links):
             turned_kri[b, m] = kri[b, m].T
+    loads[6].wait()
+    for b in each:
+        turned_fac[b] = fac[b].T
 
     away = gather(0)
     if handed:
@@ -324,11 +322,13 @@
     ]
     white = whiten(parts)
     scaled = [alpha * scaled[b] for b in each]
+    even = [alpha * white[b] for b in each]
+    less = [alpha * scaled[b] for b in each]
     columns = [
         slope_seen,
         inner([alpha * image[b] for b in each], scaled),
-        inner([whitened[b] for b in each], white) + inner(first, scaled),
-        inner(white, white) + inner(scaled, scaled),
+        inner([whitened[b] for b in each], even) + inner(first, less),
+        inner(white, even) + inner(scaled, less),
     ]
     sum_first(1, columns)
     turned = send_back(1, white)
@@ -340,13 +340,6 @@
         source_ref[b] = source[b]
         image_ref[b] = image[b]
         turned_ref[b] = turned[b] + scaled[b]
-    slope_seen, bend, mixed, last = sum_last(1, 4)
-    following = current - 2.0 * (alpha * slope_seen) + bend
-    grown = 1.0 + following / current
-    step_size = following / (grown * (grown * slope - 2.0 * mixed) + last)
-    along_ref[...] = jnp.broadcast_to(alpha + step_size * grown, (samples, width))
-    step_ref[...] = jnp.broadcast_to(step_size, (samples, width))
-
     for k in range(2):
         for up, side in near:
             halo_copy(k, up, side).wait_send()
@@ -354,7 +347,14 @@
         for side in (-1, 1):
             halo_relay(k, side).wait_send()
             back_relay(k, side).wait_send()
-        sums_sent(k)
+    sums_sent(0)
+    slope_seen, bend, mixed, last = sum_last(1, 4)
+    following = current - 2.0 * (alpha * slope_seen) + bend
+    grown = 1.0 + following / current
+    step_size = alpha * (following / (grown * (grown * current - 2.0 * mixed) + last))
+    along_ref[...] = jnp.broadcast_to(alpha + step_size * grown, (samples, width))
+    step_ref[...] = jnp.broadcast_to(step_size, (samples, width))
+    sums_sent(1)
 
 
 def body(row, rhs, precond, factor, kriging, neighbours, owner, counts):
@@ -380,6 +380,7 @@
             pltpu.SMEM(owner.shape, jnp.int32),
             pltpu.SMEM((1, 1), jnp.int32),
             pltpu.VMEM((slots, links, width, width), jnp.bfloat16),
+            pltpu.VMEM((slots, width, width), jnp.bfloat16),
             pltpu.VMEM((slots, samples, width), jnp.float32),
             pltpu.VMEM((2, 9 * slots, samples, width), jnp.bfloat16),
             pltpu.VMEM((slots * links * samples, width), jnp.bfloat16),

time: 48.9 us -> 48.8 us (level)
  no operation moved by 1% of the time
where the time goes in v5:
time: 48.8 us; the launch traced here: 48.7 us
  Pallas kernels  46.7 us (96%)
  between operations  1.29 us (3%)
  other arithmetic  0.71 us (1%)
    pallas_call x1, Pallas kernels, body(): pl.pallas_call(functools.partial(kernel, (lats, lons, row)), out_shape=(f...  46.7 us

profile of v5, /device:TPU:1, one launch (start us, length us, event | category | flops | bytes accessed | tf_op | source)
XLA Modules:
  0.0 48.7 jit_solution(9238569827768228272)
XLA Ops:
  1.3 46.7 %shard_map.86 = (f32[6,16,256]{2,1,0:T(8,128)S(1)}, f32[6,16,256]{2,1,0:T(8,128)S(1)}, f32[6,16,256]{2,1,0:T(8,128)S(1)}, f32[6,16,256]{2,1,0:T(8,128)S(1)}, f32...) custom-call(f32[6,16,256]{2,1,0:T(8,128)} %bitcast.13, f32[6,1,256]{2,1,0:T(1,128)} %bitcast.14, ...), custom_call_target="tpu_custom_call" | custom-call | tf_op jit(solution)/shard_map/pallas_call | solution.py:369
  48.0 0.7 %add_bitcast_fusion = (f32[1,1,6,16,256]{4,3,2,1,0:T(8,128)}, f32[1,1,6,16,256]{4,3,2,1,0:T(8,128)}) fusion(f32[6,16,256]{2,1,0:T(8,128)S(1)} %get-tuple-element.15, f32[6,16,256]{2,1,0:T(8,128)S(1)} %get-tuple-element.13, f32[6,16,256]{2,1,0:T(8,128)S(1)} %get-tuple-element.14, f32[16,256]{1,0:T(8,128)S(1)} %get-tuple-element.11, ...), kind=kLoop, calls=%fused_computation | loop fusion | flops 172032 | bytes 720896 | tf_op jit(solution)/shard_map/broadcast_in_dim | solution.py:422

commit v6 on v5

--- a/solution.py
+++ b/solution.py
@@ -185,10 +185,9 @@
         return [backs[b] + mine[b * samples : (b + 1) * samples] for b in range(slots)]
 
     def take_back(k, parts):
-        for up, side in near:
+        total = list(parts)
+        for up, side in near[4:] + near[2:4] + near[:2]:
             back_arrival(k, up, side).wait_recv()
-        total = list(parts)
-        for up, side in near:
             for b in range(slots):
                 piece = arrive[k, at(up, side), b * samples : (b + 1) * samples]
                 total[b] = total[b] + piece.astype(jnp.float32)

time: 48.8 us -> 48.8 us (level)
  no operation moved by 1% of the time
where the time goes in v6:
time: 48.8 us; the launch traced here: 48.7 us
  Pallas kernels  46.7 us (96%)
  between operations  1.29 us (3%)
  other arithmetic  0.71 us (1%)
    pallas_call x1, Pallas kernels, body(): pl.pallas_call(functools.partial(kernel, (lats, lons, row)), out_shape=(f...  46.7 us

profile of v6, /device:TPU:1, one launch (start us, length us, event | category | flops | bytes accessed | tf_op | source)
XLA Modules:
  0.0 48.7 jit_solution(16131642080648436621)
XLA Ops:
  1.3 46.7 %shard_map.86 = (f32[6,16,256]{2,1,0:T(8,128)S(1)}, f32[6,16,256]{2,1,0:T(8,128)S(1)}, f32[6,16,256]{2,1,0:T(8,128)S(1)}, f32[6,16,256]{2,1,0:T(8,128)S(1)}, f32...) custom-call(f32[6,16,256]{2,1,0:T(8,128)} %bitcast.13, f32[6,1,256]{2,1,0:T(1,128)} %bitcast.14, ...), custom_call_target="tpu_custom_call" | custom-call | tf_op jit(solution)/shard_map/pallas_call | solution.py:368
  47.9 0.7 %add_bitcast_fusion = (f32[1,1,6,16,256]{4,3,2,1,0:T(8,128)}, f32[1,1,6,16,256]{4,3,2,1,0:T(8,128)}) fusion(f32[6,16,256]{2,1,0:T(8,128)S(1)} %get-tuple-element.15, f32[6,16,256]{2,1,0:T(8,128)S(1)} %get-tuple-element.13, f32[6,16,256]{2,1,0:T(8,128)S(1)} %get-tuple-element.14, f32[16,256]{1,0:T(8,128)S(1)} %get-tuple-element.11, ...), kind=kLoop, calls=%fused_computation | loop fusion | flops 172032 | bytes 720896 | tf_op jit(solution)/shard_map/broadcast_in_dim | solution.py:421
